TPU v7x, 32 devices: a whole 2x2x4 slice. The times are simulated.
32 devices in a mesh: cfg: 2 (over core), req: 4 (over z), seq: 4 (over y, x).
Axes of the slice: x: 2, y: 2, z: 4, core: 2. Of those that a mesh axis runs over, the one named last changes fastest.
Arguments:
- queries: bfloat16 [2, 4, 192, 1536], P('cfg', 'req', 'seq'), may hold values from -50 to 50
- text_cache: bfloat16 [2, 4, 2, 512, 1536], P('cfg', 'req'), may hold values from -6 to 6
- image_cache: bfloat16 [2, 4, 2, 192, 1536], P('cfg', 'req'), may hold values from -6 to 6
- fresh_kv: bfloat16 [2, 4, 2, 24, 1536], P('cfg', 'req', None, 'seq'), may hold values from -6 to 6
- fresh_slots: int32 [4, 24], P('req'), may hold values from 0 to 191, as said below
- fresh_pos: int32 [3, 4, 24], P(None, 'req', 'seq'), may hold values from 0 to 63
- image_len: int32 [4], replicated, may hold values from 96 to 192, as said below
- stream: bfloat16 [2, 4, 192, 3072], P('cfg', None, 'seq', 'req'), may hold values from -30 to 30
- modulation: float32 [2, 4, 4, 3072], replicated, may hold values from -4 to 4
- out_weight: bfloat16 [1536, 3072], P('seq', 'req'), may hold values from -0.15625 to 0.15625
- up_weight: bfloat16 [3072, 12288], P('seq', 'req'), may hold values from -0.109375 to 0.109375
- down_weight: bfloat16 [12288, 3072], P('req', 'seq'), may hold values from -0.0546875 to 0.0546875
- final_weight: bfloat16 [3072, 64], replicated, may hold values from -0.109375 to 0.109375
- latent: float32 [4, 96, 128], P('req', 'seq', 'cfg'), may hold values from -6 to 6
- step_index: int32 [1], replicated, may hold values from 0 to 27
Outputs:
- latent_next: float32 [4, 96, 128], P('req', 'seq', 'cfg')
- denoised: float32 [4, 96, 128], P('req', 'seq', 'cfg')
Inputs may be any that keep to these rules, and one draw needn't show every extreme that they name: `fresh_slots`: columns k * 6 to (k + 1) * 6 - 1 of a row hold distinct slots from k * 48 to (k + 1) * 48 - 1. `image_len`: some request has exactly 192 image tokens and some other exactly 96.
All inputs are finite; a program needn't handle non-finite values.
Results may differ from a plain program's by a relative error of at most 0.0095.
Values may be sent and summed in bfloat16 or wider, within the bound.
No kernel may reach another device: no remote copies, remote signals or barrier semaphores. Data moves between devices by JAX's collectives and lax.ppermute only.
A program may use at most 128 MiB of HBM per device.

v0:
```python
import functools
import math

import jax
import jax.numpy as jnp
import numpy as np
from jax import lax
from jax.experimental import pallas as pl
from jax.experimental.pallas import tpu as pltpu
from jax.sharding import PartitionSpec as P

STEPS = 28
GUIDANCE = 3.0
SHIFT = 3.0
SCALE = 1.0 / math.sqrt(128.0)
EPSILON = 1e-06
HEAD = 128
BF16 = jnp.bfloat16
F32 = jnp.float32
MIB = 1024 * 1024


def noise_level(index):
    fraction = 1.0 - index.astype(jnp.float32) / STEPS
    return SHIFT * fraction / (SHIFT * fraction + 1.0 - fraction)


def lane_frequencies():
    rows = np.zeros((3, HEAD), np.float32)
    lane = 0
    for component, axis_span in ((0, 16), (1, 56), (2, 56)):
        pair_ids = np.arange(axis_span // 2, dtype=np.float32)
        frequency = np.exp(-(2.0 * pair_ids / axis_span) * np.float32(math.log(10000.0)))
        rows[component, lane : lane + axis_span] = np.repeat(frequency, 2)
        lane += axis_span
    return rows


def seq_grid(count):
    columns = 2 ** ((count.bit_length() - 1) // 2)
    return count // columns, columns


def send_x(block, step):
    if step == 0:
        return block
    high, wide = seq_grid(lax.axis_size("seq"))
    route = [(y * wide + x, y * wide + (x + step) % wide) for y in range(high) for x in range(wide)]
    return lax.ppermute(block, "seq", route)


def send_y(block, step):
    if step == 0:
        return block
    high, wide = seq_grid(lax.axis_size("seq"))
    route = [(y * wide + x, (y + step) % high * wide + x) for y in range(high) for x in range(wide)]
    return lax.ppermute(block, "seq", route)


def send_seq(block, dy, dx):
    if dy == 0 and dx == 0:
        return block
    high, wide = seq_grid(lax.axis_size("seq"))
    route = [
        (y * wide + x, (y + dy) % high * wide + (x + dx) % wide)
        for y in range(high)
        for x in range(wide)
    ]
    return lax.ppermute(block, "seq", route)


def send_z(block, step):
    if step == 0:
        return block
    count = lax.axis_size("req")
    return lax.ppermute(block, "req", [(r, (r + step) % count) for r in range(count)])


def swap_core(block):
    return lax.ppermute(block, "cfg", [(0, 1), (1, 0)])


def take(array, start, size, axis):
    return lax.dynamic_slice_in_dim(array, start, size, axis)


def dot(left, right):
    return jnp.dot(left, right, preferred_element_type=jnp.float32)


def hbm_spec():
    return pl.BlockSpec(memory_space=pl.ANY)


def place_of(step_x, step_y=0):
    high, wide = seq_grid(lax.axis_size("seq"))
    seq = lax.axis_index("seq")
    return lax.rem(seq // wide + high - step_y, high) * wide + x_of(step_x)


def x_of(step):
    wide = seq_grid(lax.axis_size("seq"))[1]
    return lax.rem(lax.axis_index("seq") % wide + 2 * wide - step, wide)


def z_of(step):
    count = lax.axis_size("req")
    return lax.rem(lax.axis_index("req") + count - step, count)


def whole_spec():
    return pl.BlockSpec(memory_space=pltpu.VMEM)


def smem_spec():
    return pl.BlockSpec(memory_space=pltpu.SMEM)


def cost(flops, moved):
    return pl.CostEstimate(flops=int(flops), bytes_accessed=int(moved), transcendentals=0)


def params():
    return pltpu.CompilerParams(vmem_limit_bytes=60 * MIB)


def rotate_kernel(kv_ref, pos_ref, freq_ref, out_ref):
    rows, width = kv_ref.shape[1:]
    row_ids = lax.broadcasted_iota(jnp.int32, (rows, HEAD), 0)
    angles = jnp.zeros((rows, HEAD), F32)
    for row in range(rows):
        line = (
            pos_ref[0, 0, row].astype(F32) * freq_ref[0:1, :]
            + pos_ref[1, 0, row].astype(F32) * freq_ref[1:2, :]
            + pos_ref[2, 0, row].astype(F32) * freq_ref[2:3, :]
        )
        angles = jnp.where(row_ids == row, line, angles)
    cosine, sine = jnp.cos(angles), jnp.sin(angles)
    even = lax.broadcasted_iota(jnp.int32, (rows, HEAD), 1) % 2 == 0
    out_ref[...] = jnp.zeros_like(out_ref)
    for first in range(0, width, HEAD):
        keys = kv_ref[0, :, first : first + HEAD].astype(F32)
        after = pltpu.roll(keys, HEAD - 1, 1)
        before = pltpu.roll(keys, 1, 1)
        rotated = cosine * keys + sine * jnp.where(even, -after, before)
        out_ref[0, 0:rows, first : first + HEAD] = rotated.astype(BF16)
    out_ref[1, 0:rows, :] = kv_ref[1]


def rotate_fresh(fresh, positions, padded):
    width = fresh.shape[2]
    return pl.pallas_call(
        rotate_kernel,
        out_shape=jax.ShapeDtypeStruct((2, padded, width), BF16),
        in_specs=[whole_spec(), smem_spec(), whole_spec()],
        out_specs=whole_spec(),
        compiler_params=params(),
    )(fresh, positions, jnp.asarray(lane_frequencies()))


def attention_kernel(around, lengths_ref, slots_ref, q_ref, text_ref, image_ref, *refs):
    pieces = len(around)
    fresh_refs, (out_ref, fresh_ref) = refs[:pieces], refs[pieces:]
    padded = fresh_refs[0].shape[1]
    for i in range(pieces):
        fresh_ref[:, i * padded : (i + 1) * padded, :] = fresh_refs[i][...]
    slots = image_ref.shape[1]
    count = slots_ref.shape[1] // pieces
    length = lengths_ref[lax.axis_index("req")]
    key_ids = lax.broadcasted_iota(jnp.int32, (1, slots), 1)
    fresh_ids = lax.broadcasted_iota(jnp.int32, (1, pieces * padded), 1)
    image_bias = jnp.where(key_ids < length, 0.0, -jnp.inf)
    fresh_bias = jnp.full(fresh_ids.shape, -jnp.inf, F32)
    for i, (dy, dx) in enumerate(around):
        first = place_of(dx, dy) * count
        for j in range(count):
            slot = slots_ref[0, first + j]
            image_bias = jnp.where(key_ids == slot, -jnp.inf, image_bias)
            here = (fresh_ids == i * padded + j) & (slot < length)
            fresh_bias = jnp.where(here, 0.0, fresh_bias)
    over_lanes = (((1,), (1,)), ((), ()))
    for first in range(0, q_ref.shape[1], HEAD):
        head = slice(first, first + HEAD)
        query = q_ref[:, head]

        def scores(keys):
            return lax.dot_general(query, keys, over_lanes, preferred_element_type=F32) * SCALE

        text = scores(text_ref[0, :, head])
        image = scores(image_ref[0, :, head]) + image_bias
        fresh = scores(fresh_ref[0, :, head]) + fresh_bias
        best = jnp.maximum(
            jnp.max(text, axis=1, keepdims=True),
            jnp.maximum(
                jnp.max(image, axis=1, keepdims=True), jnp.max(fresh, axis=1, keepdims=True)
            ),
        )
        text, image, fresh = jnp.exp(text - best), jnp.exp(image - best), jnp.exp(fresh - best)
        total = (
            jnp.sum(text, axis=1, keepdims=True)
            + jnp.sum(image, axis=1, keepdims=True)
            + jnp.sum(fresh, axis=1, keepdims=True)
        )
        mixed = (
            dot(text.astype(BF16), text_ref[1, :, head])
            + dot(image.astype(BF16), image_ref[1, :, head])
            + dot(fresh.astype(BF16), fresh_ref[1, :, head])
        )
        out_ref[0, :, head] = (mixed / total).astype(BF16)


def attention(around, lengths, slot_ids, query, text_kv, image_kv, fresh):
    rows, width = query.shape
    group = 3 * HEAD
    groups = width // group
    text, slots = text_kv.shape[1], image_kv.shape[1]
    pieces, padded = len(fresh), fresh[0].shape[1]
    return pl.pallas_call(
        functools.partial(attention_kernel, around),
        grid=(groups,),
        out_shape=jax.ShapeDtypeStruct((groups, rows, group), BF16),
        in_specs=[
            smem_spec(),
            smem_spec(),
            pl.BlockSpec((rows, group), lambda g: (0, g)),
            pl.BlockSpec((2, text, group), lambda g: (0, 0, g)),
            pl.BlockSpec((2, slots, group), lambda g: (0, 0, g)),
        ]
        + [pl.BlockSpec((2, padded, group), lambda g: (0, 0, g))] * pieces,
        out_specs=pl.BlockSpec((1, rows, group), lambda g: (g, 0, 0)),
        scratch_shapes=[pltpu.VMEM((2, padded * pieces, group), BF16)],
        compiler_params=params(),
    )(lengths, slot_ids, query, text_kv, image_kv, *fresh)


def residual_kernel(requests, around, *refs):
    pieces = len(around)
    attended, refs = refs[:requests], refs[requests:]
    own_ref, mine, refs = refs[0], refs[1:pieces], refs[pieces:]
    swapped_ref, stream_ref, mod_ref, out_ref, rows_ref = refs
    row_count = attended[0].shape[1]
    depth, width = own_ref.shape
    half_width = width // 2
    cfg, req = lax.axis_index("cfg"), lax.axis_index("req")
    places = [place_of(dx, dy) for dy, dx in around]
    for j in range(requests):
        first = pl.multiple_of(z_of(j) * row_count, 16)
        rows_ref[:, pl.ds(first, row_count), :] = attended[j][...]
    at = pl.multiple_of(req * width, 128)
    gates = [mod_ref[cfg, q, 0:1, pl.ds(at, width)] for q in range(requests)]

    def columns(core):
        for role, half in ((0, core), (1, 1 - core)):
            lanes = slice(half * half_width, (half + 1) * half_width)
            total = dot(rows_ref[places[0]], own_ref[:, lanes])
            for k in range(1, pieces):
                piece = swapped_ref[(k - 1) * depth : k * depth, :] if role else mine[k - 1][...]
                total += dot(rows_ref[places[k]], piece)
            for q in range(requests):
                out_ref[q, :, lanes] = (
                    stream_ref[0, q, :, lanes].astype(F32)
                    + gates[q][:, lanes] * total[q * row_count : (q + 1) * row_count]
                ).astype(BF16)

    pl.when(cfg == 0)(functools.partial(columns, 0))
    pl.when(cfg == 1)(functools.partial(columns, 1))


def residual_columns(around, attended, own, mine, swapped, stream, modulation):
    requests, pieces = len(attended), len(mine) + 1
    segments, row_count, seg = attended[0].shape
    return pl.pallas_call(
        functools.partial(residual_kernel, requests, around),
        out_shape=jax.ShapeDtypeStruct(stream.shape[1:], BF16),
        in_specs=[whole_spec()] * (requests + pieces + 3),
        out_specs=whole_spec(),
        scratch_shapes=[pltpu.VMEM((segments, requests * row_count, seg), BF16)],
        compiler_params=params(),
    )(*attended, own, *mine, swapped, stream, modulation)


def copies_of(pieces, buffer, sems):
    cfg = lax.axis_index("cfg")
    copies = []
    for k, (kind, parts) in enumerate(pieces):
        for h in range(2):
            slot = h
            if kind == "core":
                slot = cfg if h == 0 else 1 - cfg
            copies.append(
                (h, pltpu.make_async_copy(parts[h], buffer.at[slot, k], sems.at[slot, k]))
            )
    return [copy for h in range(2) for half, copy in copies if half == h]


def up_kernel(requests, around, kinds, *refs):
    blocks, refs = refs[:requests], refs[requests:]
    mod_ref, refs = refs[0], refs[1:]
    pieces = []
    for kind in kinds:
        pieces.append((kind, refs[:2]))
        refs = refs[2:]
    out_ref, own_ref, rows_ref, buffer, sems = refs
    row_count, width = blocks[0].shape[1:]
    depth, hidden = buffer.shape[2:]
    cfg, req = lax.axis_index("cfg"), lax.axis_index("req")
    scale_of_mean = 1.0 / (requests * width)
    for copy in copies_of(pieces, buffer, sems):
        copy.start()
    for q in range(requests):
        total = jnp.zeros((row_count, 1), F32)
        for block in blocks:
            total += jnp.sum(block[q].astype(F32), axis=1, keepdims=True)
        average = total * scale_of_mean
        total = jnp.zeros((row_count, 1), F32)
        for block in blocks:
            centered = block[q].astype(F32) - average
            total += jnp.sum(centered * centered, axis=1, keepdims=True)
        inverse = lax.rsqrt(total * scale_of_mean + EPSILON)
        for dz, block in enumerate(blocks):
            place = z_of(dz)
            at = pl.ds(pl.multiple_of(place * width, 128), width)
            scale = 1.0 + mod_ref[cfg, q, 2:3, at]
            shift = mod_ref[cfg, q, 1:2, at]
            normed = (block[q].astype(F32) - average) * inverse * scale + shift
            normed = normed.astype(BF16)
            for i in range(width // depth):
                rows_ref[
                    place * (width // depth) + i, q * row_count : (q + 1) * row_count, :
                ] = normed[:, i * depth : (i + 1) * depth]
    for dz, block in enumerate(blocks):
        at = pl.ds(pl.multiple_of(z_of(dz) * width, 128), width)
        own_ref[:, at] = block[req]
    step = 256 if hidden % 256 == 0 else hidden
    for h in range(2):
        for c in range(hidden // step):
            total = None
            for k, (dy, dx) in enumerate(around):
                if c == 0:
                    source = pieces[k][1][0]
                    pltpu.make_async_copy(source, buffer.at[h, k], sems.at[h, k]).wait()
                weight = buffer[h, k, :, c * step : (c + 1) * step]
                term = dot(rows_ref[place_of(dx, dy)], weight)
                total = term if total is None else total + term
            out_ref[h, :, c * step : (c + 1) * step] = jax.nn.gelu(
                total, approximate=True
            ).astype(BF16)


def up_products(around, blocks, modulation, pieces):
    requests = len(blocks)
    row_count, slice_width = blocks[0].shape[1:]
    model = requests * slice_width
    depth, hidden = pieces[0][1][0].shape[-2:]
    rows = requests * row_count
    operands = [part for _, parts in pieces for part in parts]
    return pl.pallas_call(
        functools.partial(up_kernel, requests, around, [kind for kind, _ in pieces]),
        out_shape=(
            jax.ShapeDtypeStruct((2, rows, hidden), BF16),
            jax.ShapeDtypeStruct((row_count, model), BF16),
        ),
        in_specs=[whole_spec()] * (requests + 1) + [hbm_spec()] * len(operands),
        out_specs=(whole_spec(), whole_spec()),
        scratch_shapes=[
            pltpu.VMEM((model // depth, rows, depth), BF16),
            pltpu.VMEM((2, len(pieces), depth, hidden), BF16),
            pltpu.SemaphoreType.DMA((2, len(pieces))),
        ],
        compiler_params=params(),
        cost_estimate=cost(8 * rows * model * hidden, 8 * model * hidden),
    )(*blocks, modulation, *operands)


def down_kernel(requests, wide, blocks, weights, earlier, *refs):
    acts, refs = refs[: wide * len(blocks)], refs[wide * len(blocks) :]
    weight_refs, refs = refs[:weights], refs[weights:]
    earlier_refs, refs = refs[: earlier * requests], refs[earlier * requests :]
    out_refs, (scratch_ref, buffer, sems) = refs[:requests], refs[requests:]
    rows, depth = acts[0].shape[1:]
    row_count = rows // requests
    width = buffer.shape[2]
    share = 2 * wide // weights
    for w, weight in enumerate(weight_refs):
        for i in range(share):
            slot = i
            if weights > 1:
                cfg = lax.axis_index("cfg")
                slot = (cfg if w == 0 else 1 - cfg) * share + i
            source = weight.at[pl.ds(i * depth, depth), :]
            pltpu.make_async_copy(source, buffer.at[slot], sems.at[slot]).start()
    for k, ref in enumerate(earlier_refs):
        out_refs[k % requests][len(blocks) + k // requests] = ref[0]
    step = 256 if width % 256 == 0 else width
    for c in range(width // step):
        lanes = slice(c * step, (c + 1) * step)
        total = None
        for far in range(wide):
            for h in range(2):
                slot = 2 * x_of(far) + h
                if c == 0:
                    source = weight_refs[0].at[pl.ds(0, depth), :]
                    pltpu.make_async_copy(source, buffer.at[slot], sems.at[slot]).wait()
                left = [acts[b * wide + far][h] for b in range(len(blocks))]
                left = jnp.concatenate(left, axis=0) if len(left) > 1 else left[0]
                term = dot(left, buffer[slot, :, lanes])
                total = term if total is None else total + term
        scratch_ref[...] = total
        for dz, out_ref in enumerate(out_refs):
            for b in range(len(blocks)):
                first = pl.multiple_of(b * rows + z_of(requests - dz) * row_count, 16)
                out_ref[b, :, lanes] = scratch_ref[pl.ds(first, row_count), :].astype(BF16)


def down_products(blocks, acts, weights, requests, earlier=()):
    rows, depth = acts[0].shape[1:]
    wide = math.isqrt(len(acts))
    width = weights[0].shape[1]
    step = 256 if width % 256 == 0 else width
    shape = (len(blocks) + len(earlier), rows // requests, width)
    done = [part for share in earlier for part in share]
    used = [acts[(e - far) % wide * wide + far] for e in blocks for far in range(wide)]
    return pl.pallas_call(
        functools.partial(down_kernel, requests, wide, blocks, len(weights), len(earlier)),
        out_shape=tuple(jax.ShapeDtypeStruct(shape, BF16) for _ in range(requests)),
        in_specs=[whole_spec()] * len(used)
        + [hbm_spec()] * len(weights)
        + [whole_spec()] * len(done),
        out_specs=tuple(whole_spec() for _ in range(requests)),
        scratch_shapes=[
            pltpu.VMEM((len(blocks) * rows, step), F32),
            pltpu.VMEM((2 * wide, depth, width), BF16),
            pltpu.SemaphoreType.DMA((2 * wide,)),
        ],
        compiler_params=params(),
        cost_estimate=cost(4 * len(used) * rows * depth * width, 4 * wide * depth * width),
    )(*used, *weights, *done)


def per_device(
    queries,
    text_cache,
    image_cache,
    fresh_kv,
    fresh_slots,
    fresh_pos,
    image_len,
    stream,
    modulation,
    out_weight,
    up_weight,
    down_weight,
    final_weight,
    latent,
    step_index,
):
    cfg_id = lax.axis_index("cfg")
    req_id = lax.axis_index("req")
    seq_id = lax.axis_index("seq")
    requests = lax.axis_size("req")
    high, wide = seq_grid(lax.axis_size("seq"))
    y_id, x_id = seq_id // wide, seq_id % wide
    around = [(dy, dx) for dy in range(high) for dx in range(wide)]

    def x_from(step):
        return (x_id - step) % wide

    def y_from(step):
        return (y_id - step) % high

    def seq_from(dy, dx):
        return y_from(dy) * wide + x_from(dx)

    fresh_count = fresh_kv.shape[3]
    padded = -(-fresh_count // 16) * 16
    fresh_pair = rotate_fresh(fresh_kv[0, 0], fresh_pos, padded)
    fresh = [send_seq(fresh_pair, dy, dx) for dy, dx in around]

    out_rows, col_count = out_weight.shape
    seg = col_count // 2
    own_out, _ = lax.optimization_barrier((out_weight, fresh_pair))
    own_out = take(own_out, cfg_id * seg, seg, 1)
    out_y = [send_y(own_out, dy) for dy in range(high)]
    out_x = [send_x(own_out, dx) for dx in range(wide)]

    up_rows, hidden = up_weight.shape
    hidden_x = hidden // wide
    hidden_half = hidden_x // 2
    early_up, _ = lax.optimization_barrier((up_weight, fresh_pair))
    to_x = []
    for dx in range(wide):
        first = (x_id + dx) % wide * hidden_x + cfg_id * hidden_half
        to_x.append(take(early_up, first, hidden_half, 1))
    to_x, out_x, out_y, fresh = lax.optimization_barrier((to_x, out_x, out_y, fresh))
    up_x = [send_x(part, dx) for dx, part in enumerate(to_x)]
    up_y = [send_y(up_x[0], dy) for dy in range(high)]
    out_mine = [send_y(out_x[dx], dy) if dx else out_y[dy] for dy, dx in around]

    length = lax.dynamic_index_in_dim(image_len, req_id, 0, keepdims=False)
    attended = attention(
        around,
        image_len,
        fresh_slots,
        queries[0, 0],
        text_cache[0, 0],
        image_cache[0, 0],
        fresh,
    )
    row_count = queries.shape[2]
    if attended.shape[2] != out_rows:
        attended = jnp.transpose(attended, (1, 0, 2)).reshape(row_count, -1, out_rows)
        attended = jnp.transpose(attended, (1, 0, 2))
    attended_all = [send_z(attended, dz) for dz in range(requests)]
    out_mine, attended, late_up = lax.optimization_barrier((out_mine, attended, up_weight))
    swapped = swap_core(jnp.concatenate(out_mine[1:], axis=0))
    own_up = [
        take(late_up, x_id * hidden_x + h * hidden_half, hidden_half, 1) for h in range(2)
    ]

    attended_all, swapped, up_x = lax.optimization_barrier((attended_all, swapped, up_x))
    residual = residual_columns(
        around,
        attended_all,
        out_weight,
        out_mine[1:],
        swapped,
        stream,
        modulation,
    )
    along_z = [send_z(residual, dz) for dz in range(requests)]
    near = [send_x(residual, dx) for dx in range(wide)]

    up_x[1:], _ = lax.optimization_barrier((up_x[1:], residual))
    other_y = [swap_core(part) for part in up_y[1:]]
    up_mine = [send_y(up_x[dx], dy) if dx else up_y[dy] for dy, dx in around]


    down_cols = down_weight.shape[1]
    down_half = hidden // 2
    own_down = take(down_weight, cfg_id * down_half, down_half, 0)
    along_z, near, other_y, up_mine, own_up, own_down = lax.optimization_barrier(
        (along_z, near, other_y, up_mine, own_up, own_down)
    )
    blocks = [
        [send_x(block, dx) if dz else near[dx] for dz, block in enumerate(along_z)]
        for dx in range(wide)
    ]
    down_mine = [send_y(own_down, dy) for dy in range(1, high)]
    up_pieces = [("halves", own_up)]
    for part, (dy, dx) in zip(up_mine[1:], around[1:]):
        up_pieces.append(("core", [part, swap_core(part) if dx else other_y[dy - 1]]))

    acts, own_rows = [], []
    for dx in range(wide):
        if acts:
            blocks[dx], acts[0] = lax.optimization_barrier((blocks[dx], acts[0]))
        act, own = up_products(around, blocks[dx], modulation, up_pieces)
        own_rows.append(own)
        acts += [send_x(act, step) for step in range(wide)]

    def sent(share):
        return [send_z(part, dz) for dz, part in enumerate(share)]

    earlier = []
    for e in range(1, wide):
        earlier.append(down_products([e], acts, [down_weight], requests))
        if e == 1:
            acts[-1], earlier[0] = lax.optimization_barrier((acts[-1], earlier[0]))
    share = down_products([0], acts, [down_weight], requests, earlier)
    own_share = sent(share)
    down_mine, _ = lax.optimization_barrier((down_mine, share))
    everything = list(range(wide))
    far_parts = [
        down_products(everything, acts, [mine, swap_core(mine)], requests) for mine in down_mine
    ]
    far_shares = [sent(part) for part in far_parts]
    own_share, _ = lax.optimization_barrier((own_share, far_parts))

    mod_half = lax.dynamic_index_in_dim(modulation, cfg_id, 0, keepdims=False)
    gate_two = lax.dynamic_index_in_dim(mod_half[:, 3, :], req_id, 0, keepdims=False)

    def summed(parts):
        total = parts[0].astype(F32)
        for part in parts[1:]:
            total += part.astype(F32)
        return total

    def finished(total, rows, dy):
        col = seq_from(dy, 0) * down_cols
        block_out = (
            take(rows, col, down_cols, 1).astype(F32)
            + take(gate_two, col, down_cols, 0)[None, :] * total
        ).astype(BF16)
        return dot(block_out, take(final_weight, col, down_cols, 0))

    total = summed(own_share)
    velocity = [finished(total[e], own_rows[e], 0) for e in range(wide)]
    for dy, share in enumerate(far_shares, 1):
        total = summed(share)
        for e in range(wide):
            velocity[e] += finished(total[e], own_rows[e], dy)

    channels = final_weight.shape[1]
    cfg_count = lax.axis_size("cfg")
    halves = []
    for dc in range(2):
        share = 0.0
        for e in range(wide):
            block = velocity[e].reshape(row_count // 2, 2, channels)
            block = lax.dynamic_index_in_dim(block, cfg_id ^ dc, 1, keepdims=False)
            if dc or e:
                route = [
                    ((c * high + y) * wide + x, ((c ^ dc) * high + y) * wide + (x - e) % wide)
                    for c in range(cfg_count)
                    for y in range(high)
                    for x in range(wide)
                ]
                block = lax.ppermute(block, ("cfg", "seq"), route)
            share += block
        halves.append(share)
    cond_part = jnp.where(cfg_id == 0, halves[0], halves[1])
    uncond_part = jnp.where(cfg_id == 0, halves[1], halves[0])
    guided = uncond_part + GUIDANCE * (cond_part - uncond_part)
    level_now = noise_level(step_index[0])
    level_next = noise_level(step_index[0] + 1)
    token_ids = (
        seq_id * row_count
        + 2 * jnp.arange(row_count // 2, dtype=jnp.int32)[:, None]
        + cfg_id
        + jnp.zeros((1, channels), jnp.int32)
    )
    valid = token_ids < length
    current = latent[0]
    latent_next = jnp.where(valid, current + (level_next - level_now) * guided, current)
    denoised = jnp.where(valid, current - level_now * guided, current)
    return (latent_next[None], denoised[None])


def solution(mesh):
    in_specs = (
        P("cfg", "req", "seq", None),
        P("cfg", "req", None, None, None),
        P("cfg", "req", None, None, None),
        P("cfg", "req", None, "seq", None),
        P("req", None),
        P(None, "req", "seq"),
        P(),
        P("cfg", None, "seq", "req"),
        P(),
        P("seq", "req"),
        P("seq", "req"),
        P("req", "seq"),
        P(),
        P("req", "seq", "cfg"),
        P(),
    )
    out_specs = (P("req", "seq", "cfg"), P("req", "seq", "cfg"))
    return jax.shard_map(
        per_device, mesh=mesh, in_specs=in_specs, out_specs=out_specs, check_vma=False
    )
```

profile of v0, /device:TPU:8, one launch (start us, length us, event | category | flops | bytes accessed | tf_op | source)
XLA Modules:
  0.0 177.2 jit_solution(7588983822650921299)
XLA Ops:
  4.6 1.6 collective-permute-start
  8.8 2.4 %collective-permute-start.4 = (bf16[2,16,1536]{2,1,0:T(8,128)(2,1)}, bf16[2,16,1536]{2,1,0:T(8,128)(2,1)S(1)}, u32[]{:S(2)}, u32[]{:S(2)}) collective-permute-start(bf16[2,16,1536]{2,1,0:T(8,128)(2,1)} %shard_map.167.refs_0_), channel_id=1, source_target_pairs={{0,3},{1,2},{2,1},{3,0},{4,7},{5,6},{6,5},{7,4},{8,11},{9,10},{10,... | collective-permute-start | bytes 294920 | tf_op jit(solution)/shard_map/ppermute | solution.py:69
  11.2 1.8 %constant_dynamic-slice_fusion.10 = (bf16[768,768]{1,0:T(8,128)(2,1)S(1)}, bf16[768,768]{1,0:T(8,128)(2,1)S(1)}) fusion(bf16[768,3072]{1,0:T(8,128)(2,1)} %param.26, s32[]{:T(128)S(6)} %select_n.121, s32[]{:T(128)S(6)} %select_n.119), kind=kLoop, calls=%fused_computation.56 | loop fusion | bytes 4718600 | tf_op jit(solution)/shard_map/dynamic_slice | solution.py:84
  13.0 3.6 %collective-permute-done.2.refs_1_ = bf16[2,16,1536]{2,1,0:T(8,128)(2,1)S(1)} collective-permute-done((bf16[2,16,1536]{2,1,0:T(8,128)(2,1)}, bf16[2,16,1536]{2,1,0:T(8,128)(2,1)S(1)}, u32[]{:S(2)}, u32[]{:S(2)}) %collective-permute-start.2) | collective-permute-done | bytes 98336 | tf_op jit(solution)/shard_map/ppermute | solution.py:69
  16.6 2.3 %collective-permute-done.3.refs_2_ = bf16[2,16,1536]{2,1,0:T(8,128)(2,1)S(1)} collective-permute-done((bf16[2,16,1536]{2,1,0:T(8,128)(2,1)}, bf16[2,16,1536]{2,1,0:T(8,128)(2,1)S(1)}, u32[]{:S(2)}, u32[]{:S(2)}) %collective-permute-start.3) | collective-permute-done | bytes 98336 | tf_op jit(solution)/shard_map/ppermute | solution.py:69
  18.9 1.6 collective-permute-start.8
  22.2 6.5 %shard_map.168.refs_0_ = bf16[4,48,384]{2,1,0:T(8,128)(2,1)} custom-call(s32[4]{0:T(128)} %lengths_ref.1, s32[1,24]{1,0:T(1,128)} %slots_ref.1, bf16[48,1536]{1,0:T(8,128)(2,1)} %bitcast.63, bf16[2,512,1536]{2,1,0:T(8,128)(2,1)} %bitcast.60, bf16[2,192,1536]{2,1,0:T(8,128)(2,1)} %bitcast.61, bf16[2,16,1536]{2,1,0:T(8,128)(2,1)} %shard_map.167.refs_0_, ...), custom_call_target="tpu_custom_call" | custom-call | tf_op jit(solution)/shard_map/pallas_call | solution.py:218
  29.6 1.6 collective-permute-start.5
  32.4 6.0 %collective-permute-done.5.refs_1_ = bf16[4,48,384]{2,1,0:T(8,128)(2,1)S(1)} collective-permute-done((bf16[4,48,384]{2,1,0:T(8,128)(2,1)S(1)}, bf16[4,48,384]{2,1,0:T(8,128)(2,1)S(1)}, u32[]{:S(2)}, u32[]{:S(2)}) %collective-permute-start.5) | collective-permute-done | bytes 147488 | tf_op jit(solution)/shard_map/ppermute | solution.py:76
  38.7 5.2 %collective-permute-done.6.refs_2_ = bf16[4,48,384]{2,1,0:T(8,128)(2,1)S(1)} collective-permute-done((bf16[4,48,384]{2,1,0:T(8,128)(2,1)S(1)}, bf16[4,48,384]{2,1,0:T(8,128)(2,1)S(1)}, u32[]{:S(2)}, u32[]{:S(2)}) %collective-permute-start.6) | collective-permute-done | bytes 147488 | tf_op jit(solution)/shard_map/ppermute | solution.py:76
  43.9 1.9 %collective-permute-done.7.refs_3_ = bf16[4,48,384]{2,1,0:T(8,128)(2,1)S(1)} collective-permute-done((bf16[4,48,384]{2,1,0:T(8,128)(2,1)S(1)}, bf16[4,48,384]{2,1,0:T(8,128)(2,1)S(1)}, u32[]{:S(2)}, u32[]{:S(2)}) %collective-permute-start.7) | collective-permute-done | bytes 147488 | tf_op jit(solution)/shard_map/ppermute | solution.py:76
  46.8 3.7 %shard_map.169.refs_0_ = bf16[4,48,768]{2,1,0:T(8,128)(2,1)} custom-call(bf16[4,48,384]{2,1,0:T(8,128)(2,1)} %shard_map.168.refs_0_, bf16[4,48,384]{2,1,0:T(8,128)(2,1)} %copy-done.10, bf16[4,48,384]{2,1,0:T(8,128)(2,1)} %copy-done.11, bf16[4,48,384]{2,1,0:T(8,128)(2,1)} %copy-done.12, bf16[384,768]{1,0:T(8,128)(2,1)} %refs_4_.3, ...), custom_call_target="tpu_custom_call" | custom-call | tf_op jit(solution)/shard_map/pallas_call | solution.py:272
  52.0 1.7 collective-permute-start.11
  56.3 17.6 %collective-permute-done.11.refs_1_ = bf16[4,48,768]{2,1,0:T(8,128)(2,1)} collective-permute-done((bf16[4,48,768]{2,1,0:T(8,128)(2,1)}, bf16[4,48,768]{2,1,0:T(8,128)(2,1)}, u32[]{:S(2)}, u32[]{:S(2)}) %collective-permute-start.11) | collective-permute-done | bytes 294944 | tf_op jit(solution)/shard_map/ppermute | solution.py:76
  73.8 1.7 collective-permute-start.14
  75.5 3.2 %constant_dynamic-slice_fusion.6 = bf16[1536,768]{1,0:T(8,128)(2,1)} fusion(bf16[3072,768]{1,0:T(8,128)(2,1)} %refs_2_.3, s32[]{:T(128)S(6)} %select_n.125), kind=kLoop, calls=%fused_computation.52 | loop fusion | bytes 4718596 | tf_op jit(solution)/shard_map/dynamic_slice | solution.py:84
  78.8 3.3 %constant_dynamic-slice_fusion.7 = (bf16[768,768]{1,0:T(8,128)(2,1)}, bf16[768,768]{1,0:T(8,128)(2,1)}) fusion(bf16[768,3072]{1,0:T(8,128)(2,1)} %param.26, s32[]{:T(128)S(6)} %select_n.124, s32[]{:T(128)S(6)} %select_n.123), kind=kLoop, calls=%fused_computation.53 | loop fusion | bytes 4718600 | tf_op jit(solution)/shard_map/dynamic_slice | solution.py:84
  88.6 7.5 %shard_map.170 = (bf16[2,192,768]{2,1,0:T(8,128)(2,1)}, bf16[48,3072]{1,0:T(8,128)(2,1)}) custom-call(bf16[4,48,768]{2,1,0:T(8,128)(2,1)} %shard_map.169.refs_0_, bf16[4,48,768]{2,1,0:T(8,128)(2,1)} %collective-permute-done.11.refs_1_, bf16[4,48,768]{2,1,0:T(8,128)(2,1)} %collective-permute-done.12.refs_2_, bf16[4,48,768]{2,1,0:T(8,128)(2,1)} %copy-done.25, ...), custom_call_target="tpu_custom_call" | custom-call | flops 3623878656 | bytes 18874368 | tf_op jit(solution)/shard_map/pallas_call | solution.py:357
  97.2 3.4 %collective-permute-done.21.refs_2_ = bf16[4,48,768]{2,1,0:T(8,128)(2,1)} collective-permute-done((bf16[4,48,768]{2,1,0:T(8,128)(2,1)}, bf16[4,48,768]{2,1,0:T(8,128)(2,1)}, u32[]{:S(2)}, u32[]{:S(2)}) %collective-permute-start.21) | collective-permute-done | bytes 294944 | tf_op jit(solution)/shard_map/ppermute | solution.py:49
  100.6 6.3 %collective-permute-done.22.refs_3_ = bf16[4,48,768]{2,1,0:T(8,128)(2,1)} collective-permute-done((bf16[4,48,768]{2,1,0:T(8,128)(2,1)}, bf16[4,48,768]{2,1,0:T(8,128)(2,1)}, u32[]{:S(2)}, u32[]{:S(2)}) %collective-permute-start.22) | collective-permute-done | bytes 294944 | tf_op jit(solution)/shard_map/ppermute | solution.py:49
  107.0 7.5 %shard_map.171 = (bf16[2,192,768]{2,1,0:T(8,128)(2,1)}, bf16[48,3072]{1,0:T(8,128)(2,1)}) custom-call(bf16[4,48,768]{2,1,0:T(8,128)(2,1)} %copy-done.24, bf16[4,48,768]{2,1,0:T(8,128)(2,1)} %collective-permute-done.20.refs_1_, bf16[4,48,768]{2,1,0:T(8,128)(2,1)} %collective-permute-done.21.refs_2_, bf16[4,48,768]{2,1,0:T(8,128)(2,1)} %collective-permute-done.22.refs_3_, ...), custom_call_target="tpu_custom_call" | custom-call | flops 3623878656 | bytes 18874368 | tf_op jit(solution)/shard_map/pallas_call | solution.py:357
  115.2 4.3 %collective-permute-done.24.refs_1_.refs_3_ = bf16[2,192,768]{2,1,0:T(8,128)(2,1)S(1)} collective-permute-done((bf16[2,192,768]{2,1,0:T(8,128)(2,1)}, bf16[2,192,768]{2,1,0:T(8,128)(2,1)S(1)}, u32[]{:S(2)}, u32[]{:S(2)}) %collective-permute-start.24) | collective-permute-done | bytes 589856 | tf_op jit(solution)/shard_map/ppermute | solution.py:49
  120.3 5.3 %shard_map.172 = (bf16[1,48,768]{2,1,0:T(8,128)(2,1)}, bf16[1,48,768]{2,1,0:T(8,128)(2,1)}, bf16[1,48,768]{2,1,0:T(8,128)(2,1)}, bf16[1,48,768]{2,1,0:T(8,128)(2,1)}) custom-call(bf16[2,192,768]{2,1,0:T(8,128)(2,1)} %get-tuple-element.105.refs_0_.refs_2_, bf16[2,192,768]{2,1,0:T(8,128)(2,1)} %copy-done.1, bf16[3072,768]{1,0:T(8,128)(2,1)} %refs_2_.3), custom_call_target="tpu_custom_call" | custom-call | flops 905969664 | bytes 4718592 | tf_op jit(solution)/shard_map/pallas_call | solution.py:423
  125.6 5.3 %collective-permute-done.23.refs_1_ = bf16[2,192,768]{2,1,0:T(8,128)(2,1)S(1)} collective-permute-done((bf16[2,192,768]{2,1,0:T(8,128)(2,1)}, bf16[2,192,768]{2,1,0:T(8,128)(2,1)S(1)}, u32[]{:S(2)}, u32[]{:S(2)}) %collective-permute-start.23) | collective-permute-done | bytes 589856 | tf_op jit(solution)/shard_map/ppermute | solution.py:49
  131.7 5.5 %shard_map.173 = (bf16[2,48,768]{2,1,0:T(8,128)(2,1)}, bf16[2,48,768]{2,1,0:T(8,128)(2,1)}, bf16[2,48,768]{2,1,0:T(8,128)(2,1)}, bf16[2,48,768]{2,1,0:T(8,128)(2,1)}) custom-call(bf16[2,192,768]{2,1,0:T(8,128)(2,1)} %get-tuple-element.100.refs_0_, bf16[2,192,768]{2,1,0:T(8,128)(2,1)} %copy-done.2, bf16[3072,768]{1,0:T(8,128)(2,1)} %refs_2_.3, ...), custom_call_target="tpu_custom_call" | custom-call | flops 905969664 | bytes 4718592 | tf_op jit(solution)/shard_map/pallas_call | solution.py:423
  138.2 3.0 %collective-permute-start.25 = (bf16[2,48,768]{2,1,0:T(8,128)(2,1)}, bf16[2,48,768]{2,1,0:T(8,128)(2,1)S(1)}, u32[]{:S(2)}, u32[]{:S(2)}) collective-permute-start(bf16[2,48,768]{2,1,0:T(8,128)(2,1)} %get-tuple-element.116), channel_id=1, source_target_pairs={{0,4},{4,8},{8,12},{12,0},{1,5},{5,9},{9,13},{13,1},{2,6},{6,10},{... | collective-permute-start | bytes 442376 | tf_op jit(solution)/shard_map/ppermute | solution.py:76
  144.1 6.9 %shard_map.174 = (bf16[2,48,768]{2,1,0:T(8,128)(2,1)}, bf16[2,48,768]{2,1,0:T(8,128)(2,1)}, bf16[2,48,768]{2,1,0:T(8,128)(2,1)}, bf16[2,48,768]{2,1,0:T(8,128)(2,1)}) custom-call(bf16[2,192,768]{2,1,0:T(8,128)(2,1)} %get-tuple-element.100.refs_0_, bf16[2,192,768]{2,1,0:T(8,128)(2,1)} %copy-done.2, bf16[2,192,768]{2,1,0:T(8,128)(2,1)} %get-tuple-element.105.refs_0_.refs_2_, ...), custom_call_target="tpu_custom_call" | custom-call | flops 1811939328 | bytes 4718592 | tf_op jit(solution)/shard_map/pallas_call | solution.py:423
  151.1 2.3 %collective-permute-start.30 = (bf16[2,48,768]{2,1,0:T(8,128)(2,1)}, bf16[2,48,768]{2,1,0:T(8,128)(2,1)S(1)}, u32[]{:S(2)}, u32[]{:S(2)}) collective-permute-start(bf16[2,48,768]{2,1,0:T(8,128)(2,1)} %get-tuple-element.122), channel_id=1, source_target_pairs={{0,4},{4,8},{8,12},{12,0},{1,5},{5,9},{9,13},{13,1},{2,6},{6,10},{... | collective-permute-start | bytes 442376 | tf_op jit(solution)/shard_map/ppermute | solution.py:76
  153.4 3.0 %collective-permute-start.31 = (bf16[2,48,768]{2,1,0:T(8,128)(2,1)}, bf16[2,48,768]{2,1,0:T(8,128)(2,1)S(1)}, u32[]{:S(2)}, u32[]{:S(2)}) collective-permute-start(bf16[2,48,768]{2,1,0:T(8,128)(2,1)} %get-tuple-element.123), channel_id=1, source_target_pairs={{0,8},{4,12},{8,0},{12,4},{1,9},{5,13},{9,1},{13,5},{2,10},{6,14},... | collective-permute-start | bytes 442376 | tf_op jit(solution)/shard_map/ppermute | solution.py:76
  156.8 2.0 %collective-permute-done.30 = bf16[2,48,768]{2,1,0:T(8,128)(2,1)S(1)} collective-permute-done((bf16[2,48,768]{2,1,0:T(8,128)(2,1)}, bf16[2,48,768]{2,1,0:T(8,128)(2,1)S(1)}, u32[]{:S(2)}, u32[]{:S(2)}) %collective-permute-start.30) | collective-permute-done | bytes 147488 | tf_op jit(solution)/shard_map/ppermute | solution.py:76
  158.8 8.5 %collective-permute-done.31 = bf16[2,48,768]{2,1,0:T(8,128)(2,1)S(1)} collective-permute-done((bf16[2,48,768]{2,1,0:T(8,128)(2,1)}, bf16[2,48,768]{2,1,0:T(8,128)(2,1)S(1)}, u32[]{:S(2)}, u32[]{:S(2)}) %collective-permute-start.31) | collective-permute-done | bytes 147488 | tf_op jit(solution)/shard_map/ppermute | solution.py:76
  167.3 2.0 %collective-permute-done.32 = bf16[2,48,768]{2,1,0:T(8,128)(2,1)S(1)} collective-permute-done((bf16[2,48,768]{2,1,0:T(8,128)(2,1)}, bf16[2,48,768]{2,1,0:T(8,128)(2,1)S(1)}, u32[]{:S(2)}, u32[]{:S(2)}) %collective-permute-start.32) | collective-permute-done | bytes 147488 | tf_op jit(solution)/shard_map/ppermute | solution.py:76
  (120 shorter events, 36.9 us)
Async XLA Ops:
  4.6 14.2 %collective-permute-start = (bf16[384,384]{1,0:T(8,128)(2,1)S(1)}, bf16[384,384]{1,0:T(8,128)(2,1)S(1)}, u32[]{:S(2)}, u32[]{:S(2)}) collective-permute-start(bf16[384,384]{1,0:T(8,128)(2,1)S(1)} %constant_dynamic-slice_fusion.9), channel_id=1, source_target_pairs={{0,1},{1,0},{2,3},{3,2},{4,5},{5,4},{6,7},{7,6},{8,9},{9,8},{10,11... | collective-permute-start | bytes 884744 | tf_op jit(solution)/shard_map/ppermute | solution.py:49
  6.2 12.7 %collective-permute-start.1 = (bf16[384,384]{1,0:T(8,128)(2,1)S(1)}, bf16[384,384]{1,0:T(8,128)(2,1)S(1)}, u32[]{:S(2)}, u32[]{:S(2)}) collective-permute-start(bf16[384,384]{1,0:T(8,128)(2,1)S(1)} %constant_dynamic-slice_fusion.9), channel_id=1, source_target_pairs={{0,2},{1,3},{2,0},{3,1},{4,6},{5,7},{6,4},{7,5},{8,10},{9,11},{10,... | collective-permute-start | bytes 884744 | tf_op jit(solution)/shard_map/ppermute | solution.py:57
  7.7 8.9 %collective-permute-start.2 = (bf16[2,16,1536]{2,1,0:T(8,128)(2,1)}, bf16[2,16,1536]{2,1,0:T(8,128)(2,1)S(1)}, u32[]{:S(2)}, u32[]{:S(2)}) collective-permute-start(bf16[2,16,1536]{2,1,0:T(8,128)(2,1)} %shard_map.167.refs_0_), channel_id=1, source_target_pairs={{0,1},{1,0},{2,3},{3,2},{4,5},{5,4},{6,7},{7,6},{8,9},{9,8},{10,11... | collective-permute-start | bytes 294920 | tf_op jit(solution)/shard_map/ppermute | solution.py:69
  8.2 10.6 %collective-permute-start.3 = (bf16[2,16,1536]{2,1,0:T(8,128)(2,1)}, bf16[2,16,1536]{2,1,0:T(8,128)(2,1)S(1)}, u32[]{:S(2)}, u32[]{:S(2)}) collective-permute-start(bf16[2,16,1536]{2,1,0:T(8,128)(2,1)} %shard_map.167.refs_0_), channel_id=1, source_target_pairs={{0,2},{1,3},{2,0},{3,1},{4,6},{5,7},{6,4},{7,5},{8,10},{9,11},{10,... | collective-permute-start | bytes 294920 | tf_op jit(solution)/shard_map/ppermute | solution.py:69
  8.8 10.1 %collective-permute-start.4 = (bf16[2,16,1536]{2,1,0:T(8,128)(2,1)}, bf16[2,16,1536]{2,1,0:T(8,128)(2,1)S(1)}, u32[]{:S(2)}, u32[]{:S(2)}) collective-permute-start(bf16[2,16,1536]{2,1,0:T(8,128)(2,1)} %shard_map.167.refs_0_), channel_id=1, source_target_pairs={{0,3},{1,2},{2,1},{3,0},{4,7},{5,6},{6,5},{7,4},{8,11},{9,10},{10,... | collective-permute-start | bytes 294920 | tf_op jit(solution)/shard_map/ppermute | solution.py:69
  18.9 10.0 %collective-permute-start.8 = (bf16[384,384]{1,0:T(8,128)(2,1)S(1)}, bf16[384,384]{1,0:T(8,128)(2,1)S(1)}, u32[]{:S(2)}, u32[]{:S(2)}) collective-permute-start(bf16[384,384]{1,0:T(8,128)(2,1)S(1)} %collective-permute-done.refs_5_), channel_id=1, source_target_pairs={{0,2},{1,3},{2,0},{3,1},{4,6},{5,7},{6,4},{7,5},{8,10},{9,11},{10,... | collective-permute-start | bytes 884744 | tf_op jit(solution)/shard_map/ppermute | solution.py:57
  20.5 26.3 %collective-permute-start.10 = (bf16[768,768]{1,0:T(8,128)(2,1)S(1)}, bf16[768,768]{1,0:T(8,128)(2,1)}, u32[]{:S(2)}, u32[]{:S(2)}) collective-permute-start(bf16[768,768]{1,0:T(8,128)(2,1)S(1)} %get-tuple-element.78), channel_id=1, source_target_pairs={{0,1},{1,0},{2,3},{3,2},{4,5},{5,4},{6,7},{7,6},{8,9},{9,8},{10,11... | collective-permute-start | bytes 3538952 | tf_op jit(solution)/shard_map/ppermute | solution.py:49
  21.0 30.9 %collective-permute-start.15 = (bf16[768,768]{1,0:T(8,128)(2,1)S(1)}, bf16[768,768]{1,0:T(8,128)(2,1)}, u32[]{:S(2)}, u32[]{:S(2)}) collective-permute-start(bf16[768,768]{1,0:T(8,128)(2,1)S(1)} %get-tuple-element.77), channel_id=1, source_target_pairs={{0,2},{1,3},{2,0},{3,1},{4,6},{5,7},{6,4},{7,5},{8,10},{9,11},{10,... | collective-permute-start | bytes 3538952 | tf_op jit(solution)/shard_map/ppermute | solution.py:57
  29.0 16.8 %collective-permute-start.9 = (bf16[1152,384]{1,0:T(8,128)(2,1)S(1)}, bf16[1152,384]{1,0:T(8,128)(2,1)S(1)}, u32[]{:S(2)}, u32[]{:S(2)}) collective-permute-start(bf16[1152,384]{1,0:T(8,128)(2,1)S(1)} %pad_maximum_fusion), channel_id=1, source_target_pairs={{0,16},{16,0},{1,17},{17,1},{2,18},{18,2},{3,19},{19,3},{4,20},{20... | collective-permute-start | bytes 2654216 | tf_op jit(solution)/shard_map/ppermute | solution.py:80
  29.6 8.8 %collective-permute-start.5 = (bf16[4,48,384]{2,1,0:T(8,128)(2,1)S(1)}, bf16[4,48,384]{2,1,0:T(8,128)(2,1)S(1)}, u32[]{:S(2)}, u32[]{:S(2)}) collective-permute-start(bf16[4,48,384]{2,1,0:T(8,128)(2,1)S(1)} %copy-done.9), channel_id=1, source_target_pairs={{0,4},{4,8},{8,12},{12,0},{1,5},{5,9},{9,13},{13,1},{2,6},{6,10},{... | collective-permute-start | bytes 442376 | tf_op jit(solution)/shard_map/ppermute | solution.py:76
  31.2 12.7 %collective-permute-start.6 = (bf16[4,48,384]{2,1,0:T(8,128)(2,1)S(1)}, bf16[4,48,384]{2,1,0:T(8,128)(2,1)S(1)}, u32[]{:S(2)}, u32[]{:S(2)}) collective-permute-start(bf16[4,48,384]{2,1,0:T(8,128)(2,1)S(1)} %copy-done.9), channel_id=1, source_target_pairs={{0,8},{4,12},{8,0},{12,4},{1,9},{5,13},{9,1},{13,5},{2,10},{6,14},... | collective-permute-start | bytes 442376 | tf_op jit(solution)/shard_map/ppermute | solution.py:76
  38.5 7.3 %collective-permute-start.7 = (bf16[4,48,384]{2,1,0:T(8,128)(2,1)S(1)}, bf16[4,48,384]{2,1,0:T(8,128)(2,1)S(1)}, u32[]{:S(2)}, u32[]{:S(2)}) collective-permute-start(bf16[4,48,384]{2,1,0:T(8,128)(2,1)S(1)} %copy-done.9), channel_id=1, source_target_pairs={{0,12},{4,0},{8,4},{12,8},{1,13},{5,1},{9,5},{13,9},{2,14},{6,2},{... | collective-permute-start | bytes 442376 | tf_op jit(solution)/shard_map/ppermute | solution.py:76
  50.5 31.5 %collective-permute-start.17 = (bf16[768,768]{1,0:T(8,128)(2,1)}, bf16[768,768]{1,0:T(8,128)(2,1)S(1)}, u32[]{:S(2)}, u32[]{:S(2)}) collective-permute-start(bf16[768,768]{1,0:T(8,128)(2,1)} %collective-permute-done.10.refs_7_), channel_id=1, source_target_pairs={{0,2},{1,3},{2,0},{3,1},{4,6},{5,7},{6,4},{7,5},{8,10},{9,11},{10,... | collective-permute-start | bytes 3538952 | tf_op jit(solution)/shard_map/ppermute | solution.py:57
  52.0 30.1 %collective-permute-start.16 = (bf16[768,768]{1,0:T(8,128)(2,1)}, bf16[768,768]{1,0:T(8,128)(2,1)S(1)}, u32[]{:S(2)}, u32[]{:S(2)}) collective-permute-start(bf16[768,768]{1,0:T(8,128)(2,1)} %collective-permute-done.15.refs_9_), channel_id=1, source_target_pairs={{0,16},{16,0},{1,17},{17,1},{2,18},{18,2},{3,19},{19,3},{4,20},{20... | collective-permute-start | bytes 3538952 | tf_op jit(solution)/shard_map/ppermute | solution.py:80
  52.0 21.9 %collective-permute-start.11 = (bf16[4,48,768]{2,1,0:T(8,128)(2,1)}, bf16[4,48,768]{2,1,0:T(8,128)(2,1)}, u32[]{:S(2)}, u32[]{:S(2)}) collective-permute-start(bf16[4,48,768]{2,1,0:T(8,128)(2,1)} %shard_map.169.refs_0_), channel_id=1, source_target_pairs={{0,4},{4,8},{8,12},{12,0},{1,5},{5,9},{9,13},{13,1},{2,6},{6,10},{... | collective-permute-start | bytes 884744 | tf_op jit(solution)/shard_map/ppermute | solution.py:76
  53.7 28.3 %collective-permute-start.12 = (bf16[4,48,768]{2,1,0:T(8,128)(2,1)}, bf16[4,48,768]{2,1,0:T(8,128)(2,1)}, u32[]{:S(2)}, u32[]{:S(2)}) collective-permute-start(bf16[4,48,768]{2,1,0:T(8,128)(2,1)} %shard_map.169.refs_0_), channel_id=1, source_target_pairs={{0,8},{4,12},{8,0},{12,4},{1,9},{5,13},{9,1},{13,5},{2,10},{6,14},... | collective-permute-start | bytes 884744 | tf_op jit(solution)/shard_map/ppermute | solution.py:76
  54.9 27.2 %collective-permute-start.13 = (bf16[4,48,768]{2,1,0:T(8,128)(2,1)}, bf16[4,48,768]{2,1,0:T(8,128)(2,1)S(1)}, u32[]{:S(2)}, u32[]{:S(2)}) collective-permute-start(bf16[4,48,768]{2,1,0:T(8,128)(2,1)} %shard_map.169.refs_0_), channel_id=1, source_target_pairs={{0,12},{4,0},{8,4},{12,8},{1,13},{5,1},{9,5},{13,9},{2,14},{6,2},{... | collective-permute-start | bytes 884744 | tf_op jit(solution)/shard_map/ppermute | solution.py:76
  73.8 8.2 %collective-permute-start.14 = (bf16[4,48,768]{2,1,0:T(8,128)(2,1)}, bf16[4,48,768]{2,1,0:T(8,128)(2,1)S(1)}, u32[]{:S(2)}, u32[]{:S(2)}) collective-permute-start(bf16[4,48,768]{2,1,0:T(8,128)(2,1)} %shard_map.169.refs_0_), channel_id=1, source_target_pairs={{0,1},{1,0},{2,3},{3,2},{4,5},{5,4},{6,7},{7,6},{8,9},{9,8},{10,11... | collective-permute-start | bytes 884744 | tf_op jit(solution)/shard_map/ppermute | solution.py:49
  82.8 4.9 %collective-permute-start.19 = (bf16[768,768]{1,0:T(8,128)(2,1)S(1)}, bf16[768,768]{1,0:T(8,128)(2,1)}, u32[]{:S(2)}, u32[]{:S(2)}) collective-permute-start(bf16[768,768]{1,0:T(8,128)(2,1)S(1)} %collective-permute-done.17.refs_11_), channel_id=1, source_target_pairs={{0,16},{16,0},{1,17},{17,1},{2,18},{18,2},{3,19},{19,3},{4,20},{20... | collective-permute-start | bytes 3538952 | tf_op jit(solution)/shard_map/ppermute | solution.py:80
  83.4 53.9 %collective-permute-start.28 = (bf16[1536,768]{1,0:T(8,128)(2,1)}, bf16[1536,768]{1,0:T(8,128)(2,1)}, u32[]{:S(2)}, u32[]{:S(2)}) collective-permute-start(bf16[1536,768]{1,0:T(8,128)(2,1)} %constant_dynamic-slice_fusion.6), channel_id=1, source_target_pairs={{0,2},{1,3},{2,0},{3,1},{4,6},{5,7},{6,4},{7,5},{8,10},{9,11},{10,... | collective-permute-start | bytes 7077896 | tf_op jit(solution)/shard_map/ppermute | solution.py:57
  84.1 13.1 %collective-permute-start.20 = (bf16[4,48,768]{2,1,0:T(8,128)(2,1)}, bf16[4,48,768]{2,1,0:T(8,128)(2,1)}, u32[]{:S(2)}, u32[]{:S(2)}) collective-permute-start(bf16[4,48,768]{2,1,0:T(8,128)(2,1)} %collective-permute-done.11.refs_1_), channel_id=1, source_target_pairs={{0,1},{1,0},{2,3},{3,2},{4,5},{5,4},{6,7},{7,6},{8,9},{9,8},{10,11... | collective-permute-start | bytes 884744 | tf_op jit(solution)/shard_map/ppermute | solution.py:49
  84.7 15.9 %collective-permute-start.21 = (bf16[4,48,768]{2,1,0:T(8,128)(2,1)}, bf16[4,48,768]{2,1,0:T(8,128)(2,1)}, u32[]{:S(2)}, u32[]{:S(2)}) collective-permute-start(bf16[4,48,768]{2,1,0:T(8,128)(2,1)} %collective-permute-done.12.refs_2_), channel_id=1, source_target_pairs={{0,1},{1,0},{2,3},{3,2},{4,5},{5,4},{6,7},{7,6},{8,9},{9,8},{10,11... | collective-permute-start | bytes 884744 | tf_op jit(solution)/shard_map/ppermute | solution.py:49
  87.6 19.4 %collective-permute-start.22 = (bf16[4,48,768]{2,1,0:T(8,128)(2,1)}, bf16[4,48,768]{2,1,0:T(8,128)(2,1)}, u32[]{:S(2)}, u32[]{:S(2)}) collective-permute-start(bf16[4,48,768]{2,1,0:T(8,128)(2,1)} %copy-done.25), channel_id=1, source_target_pairs={{0,1},{1,0},{2,3},{3,2},{4,5},{5,4},{6,7},{7,6},{8,9},{9,8},{10,11... | collective-permute-start | bytes 884744 | tf_op jit(solution)/shard_map/ppermute | solution.py:49
  96.1 23.4 %collective-permute-start.24 = (bf16[2,192,768]{2,1,0:T(8,128)(2,1)}, bf16[2,192,768]{2,1,0:T(8,128)(2,1)S(1)}, u32[]{:S(2)}, u32[]{:S(2)}) collective-permute-start(bf16[2,192,768]{2,1,0:T(8,128)(2,1)} %get-tuple-element.100.refs_0_), channel_id=1, source_target_pairs={{0,1},{1,0},{2,3},{3,2},{4,5},{5,4},{6,7},{7,6},{8,9},{9,8},{10,11... | collective-permute-start | bytes 1769480 | tf_op jit(solution)/shard_map/ppermute | solution.py:49
  114.5 16.4 %collective-permute-start.23 = (bf16[2,192,768]{2,1,0:T(8,128)(2,1)}, bf16[2,192,768]{2,1,0:T(8,128)(2,1)S(1)}, u32[]{:S(2)}, u32[]{:S(2)}) collective-permute-start(bf16[2,192,768]{2,1,0:T(8,128)(2,1)} %get-tuple-element.105.refs_0_.refs_2_), channel_id=1, source_target_pairs={{0,1},{1,0},{2,3},{3,2},{4,5},{5,4},{6,7},{7,6},{8,9},{9,8},{10,11... | collective-permute-start | bytes 1769480 | tf_op jit(solution)/shard_map/ppermute | solution.py:49
  137.2 5.5 %collective-permute-start.29 = (bf16[1536,768]{1,0:T(8,128)(2,1)}, bf16[1536,768]{1,0:T(8,128)(2,1)S(1)}, u32[]{:S(2)}, u32[]{:S(2)}) collective-permute-start(bf16[1536,768]{1,0:T(8,128)(2,1)} %collective-permute-done.28.refs_4_), channel_id=1, source_target_pairs={{0,16},{16,0},{1,17},{17,1},{2,18},{18,2},{3,19},{19,3},{4,20},{20... | collective-permute-start | bytes 7077896 | tf_op jit(solution)/shard_map/ppermute | solution.py:80
  138.2 18.2 %collective-permute-start.25 = (bf16[2,48,768]{2,1,0:T(8,128)(2,1)}, bf16[2,48,768]{2,1,0:T(8,128)(2,1)S(1)}, u32[]{:S(2)}, u32[]{:S(2)}) collective-permute-start(bf16[2,48,768]{2,1,0:T(8,128)(2,1)} %get-tuple-element.116), channel_id=1, source_target_pairs={{0,4},{4,8},{8,12},{12,0},{1,5},{5,9},{9,13},{13,1},{2,6},{6,10},{... | collective-permute-start | bytes 442376 | tf_op jit(solution)/shard_map/ppermute | solution.py:76
  141.2 15.2 %collective-permute-start.26 = (bf16[2,48,768]{2,1,0:T(8,128)(2,1)}, bf16[2,48,768]{2,1,0:T(8,128)(2,1)S(1)}, u32[]{:S(2)}, u32[]{:S(2)}) collective-permute-start(bf16[2,48,768]{2,1,0:T(8,128)(2,1)} %get-tuple-element.117), channel_id=1, source_target_pairs={{0,8},{4,12},{8,0},{12,4},{1,9},{5,13},{9,1},{13,5},{2,10},{6,14},... | collective-permute-start | bytes 442376 | tf_op jit(solution)/shard_map/ppermute | solution.py:76
  141.2 15.2 %collective-permute-start.27 = (bf16[2,48,768]{2,1,0:T(8,128)(2,1)}, bf16[2,48,768]{2,1,0:T(8,128)(2,1)S(1)}, u32[]{:S(2)}, u32[]{:S(2)}) collective-permute-start(bf16[2,48,768]{2,1,0:T(8,128)(2,1)} %get-tuple-element.118), channel_id=1, source_target_pairs={{0,12},{4,0},{8,4},{12,8},{1,13},{5,1},{9,5},{13,9},{2,14},{6,2},{... | collective-permute-start | bytes 442376 | tf_op jit(solution)/shard_map/ppermute | solution.py:76
  151.1 7.7 %collective-permute-start.30 = (bf16[2,48,768]{2,1,0:T(8,128)(2,1)}, bf16[2,48,768]{2,1,0:T(8,128)(2,1)S(1)}, u32[]{:S(2)}, u32[]{:S(2)}) collective-permute-start(bf16[2,48,768]{2,1,0:T(8,128)(2,1)} %get-tuple-element.122), channel_id=1, source_target_pairs={{0,4},{4,8},{8,12},{12,0},{1,5},{5,9},{9,13},{13,1},{2,6},{6,10},{... | collective-permute-start | bytes 442376 | tf_op jit(solution)/shard_map/ppermute | solution.py:76
  153.4 13.9 %collective-permute-start.31 = (bf16[2,48,768]{2,1,0:T(8,128)(2,1)}, bf16[2,48,768]{2,1,0:T(8,128)(2,1)S(1)}, u32[]{:S(2)}, u32[]{:S(2)}) collective-permute-start(bf16[2,48,768]{2,1,0:T(8,128)(2,1)} %get-tuple-element.123), channel_id=1, source_target_pairs={{0,8},{4,12},{8,0},{12,4},{1,9},{5,13},{9,1},{13,5},{2,10},{6,14},... | collective-permute-start | bytes 442376 | tf_op jit(solution)/shard_map/ppermute | solution.py:76
  156.4 12.9 %collective-permute-start.32 = (bf16[2,48,768]{2,1,0:T(8,128)(2,1)}, bf16[2,48,768]{2,1,0:T(8,128)(2,1)S(1)}, u32[]{:S(2)}, u32[]{:S(2)}) collective-permute-start(bf16[2,48,768]{2,1,0:T(8,128)(2,1)} %get-tuple-element.124), channel_id=1, source_target_pairs={{0,12},{4,0},{8,4},{12,8},{1,13},{5,1},{9,5},{13,9},{2,14},{6,2},{... | collective-permute-start | bytes 442376 | tf_op jit(solution)/shard_map/ppermute | solution.py:76
  (30 other events, 343.9 us)
where the time goes:
time: 178 us; the launch traced here: 177 us
  waiting for transfers between devices  71.6 us (40%)
  Pallas kernels  44.5 us (25%)
  starting transfers between devices  37.7 us (21%)
  local copies, waits for them, and re-layouts  17.7 us (10%)
  other arithmetic  3.15 us (2%)
  between operations  1.88 us (1%)
    ppermute x12, waiting for transfers between devices, send_z(): lax.ppermute(block, 'req', [(r, (r + step) % count) for r in range(count)])  43.2 us
    ppermute x8, waiting for transfers between devices, send_x(): return lax.ppermute(block, 'seq', route)  19.4 us
    pallas_call x3, Pallas kernels, down_products(): pl.pallas_call(functools.partial(down_kernel, requests, wide, blocks, len...  17.7 us
    ppermute x12, starting transfers between devices, send_z(): lax.ppermute(block, 'req', [(r, (r + step) % count) for r in range(count)])  17.1 us
    pallas_call x2, Pallas kernels, up_products(): pl.pallas_call(functools.partial(up_kernel, requests, around, [kind for k...  15 us
    dynamic_slice x5, local copies, waits for them, and re-layouts, take(): return lax.dynamic_slice_in_dim(array, start, size, axis)  9.35 us
    ppermute x8, starting transfers between devices, send_x(): return lax.ppermute(block, 'seq', route)  7.77 us
    unnamed x53, local copies, waits for them, and re-layouts  7.65 us
  transfers between devices with their start and end apart: 36, of which 16 were waited for; matrix products, arithmetic and copies ran while one was open for 6% of the time, Pallas kernels for 24%

commit v1 on v0

--- a/solution.py
+++ b/solution.py
@@ -517,7 +517,9 @@
         take(late_up, x_id * hidden_x + h * hidden_half, hidden_half, 1) for h in range(2)
     ]
 
-    attended_all, swapped, up_x = lax.optimization_barrier((attended_all, swapped, up_x))
+    attended_all, swapped, up_x, own_up = lax.optimization_barrier(
+        (attended_all, swapped, up_x, own_up)
+    )
     residual = residual_columns(
         around,
         attended_all,
@@ -534,12 +536,11 @@
     other_y = [swap_core(part) for part in up_y[1:]]
     up_mine = [send_y(up_x[dx], dy) if dx else up_y[dy] for dy, dx in around]
 
-
     down_cols = down_weight.shape[1]
     down_half = hidden // 2
     own_down = take(down_weight, cfg_id * down_half, down_half, 0)
-    along_z, near, other_y, up_mine, own_up, own_down = lax.optimization_barrier(
-        (along_z, near, other_y, up_mine, own_up, own_down)
+    along_z, near, other_y, up_mine, own_down = lax.optimization_barrier(
+        (along_z, near, other_y, up_mine, own_down)
     )
     blocks = [
         [send_x(block, dx) if dz else near[dx] for dz, block in enumerate(along_z)]

time: 178 us -> 176 us (0.989)
  waiting for transfers between devices: 71.6 us -> 62.6 us
  starting transfers between devices: 37.7 us -> 46 us
    ppermute x8, starting transfers between devices: 7.77 us -> 20 us  [send_x(): return lax.ppermute(block, 'seq', route)]
    ppermute x12, waiting for transfers between devices: 43.2 us -> 33.5 us  [send_z(): lax.ppermute(block, 'req', [(r, (r + step) % count) for r in range(count)])]
    ppermute x12, starting transfers between devices: 17.1 us -> 13.3 us  [send_z(): lax.ppermute(block, 'req', [(r, (r + step) % count) for r in range(count)])]
    unnamed x53 -> x49, local copies, waits for them, and re-layouts: 7.65 us -> 5.23 us
  transfers between devices with their start and end apart: 36 -> 36, of which waited for: 16 -> 20; matrix products, arithmetic and copies ran while one was open for 6% -> 6% of each run, Pallas kernels for 24% -> 24%
where the time goes in v1:
time: 176 us
  waiting for transfers between devices  62.6 us (36%)
  starting transfers between devices  46 us (26%)
  Pallas kernels  44.5 us (25%)
  local copies, waits for them, and re-layouts  16 us (9%)
  other arithmetic  4.08 us (2%)
  between operations  1.84 us (1%)
    ppermute x12, waiting for transfers between devices, send_z(): lax.ppermute(block, 'req', [(r, (r + step) % count) for r in range(count)])  33.5 us
    ppermute x8, starting transfers between devices, send_x(): return lax.ppermute(block, 'seq', route)  20 us
    ppermute x8, waiting for transfers between devices, send_x(): return lax.ppermute(block, 'seq', route)  18.9 us
    pallas_call x3, Pallas kernels, down_products(): pl.pallas_call(functools.partial(down_kernel, requests, wide, blocks, len...  17.7 us
    pallas_call x2, Pallas kernels, up_products(): pl.pallas_call(functools.partial(up_kernel, requests, around, [kind for k...  15 us
    ppermute x12, starting transfers between devices, send_z(): lax.ppermute(block, 'req', [(r, (r + step) % count) for r in range(count)])  13.3 us
    dynamic_slice x5, local copies, waits for them, and re-layouts, take(): return lax.dynamic_slice_in_dim(array, start, size, axis)  10.1 us
    pallas_call x1, Pallas kernels, attention(): pl.pallas_call(functools.partial(attention_kernel, around), grid=(groups,...  6.49 us
  transfers between devices with their start and end apart: 36, of which 20 were waited for; matrix products, arithmetic and copies ran while one was open for 6% of the time, Pallas kernels for 24%

profile of v1, /device:TPU:8, one launch (start us, length us, event | category | flops | bytes accessed | tf_op | source)
XLA Modules:
  0.0 175.7 jit_solution(2960024700012977744)
XLA Ops:
  3.7 1.7 constant_dynamic-slice_fusion.9
  9.4 2.4 %collective-permute-start.4 = (bf16[2,16,1536]{2,1,0:T(8,128)(2,1)}, bf16[2,16,1536]{2,1,0:T(8,128)(2,1)}, u32[]{:S(2)}, u32[]{:S(2)}) collective-permute-start(bf16[2,16,1536]{2,1,0:T(8,128)(2,1)} %shard_map.167.refs_0_), channel_id=1, source_target_pairs={{0,3},{1,2},{2,1},{3,0},{4,7},{5,6},{6,5},{7,4},{8,11},{9,10},{10,... | collective-permute-start | bytes 294920 | tf_op jit(solution)/shard_map/ppermute | solution.py:69
  11.9 1.8 %constant_dynamic-slice_fusion.10 = (bf16[768,768]{1,0:T(8,128)(2,1)S(1)}, bf16[768,768]{1,0:T(8,128)(2,1)S(1)}) fusion(bf16[768,3072]{1,0:T(8,128)(2,1)} %param.26, s32[]{:T(128)S(6)} %select_n.121, s32[]{:T(128)S(6)} %select_n.119), kind=kLoop, calls=%fused_computation.56 | loop fusion | bytes 4718600 | tf_op jit(solution)/shard_map/dynamic_slice | solution.py:84
  13.7 3.8 %collective-permute-done.2.refs_1_ = bf16[2,16,1536]{2,1,0:T(8,128)(2,1)S(1)} collective-permute-done((bf16[2,16,1536]{2,1,0:T(8,128)(2,1)}, bf16[2,16,1536]{2,1,0:T(8,128)(2,1)S(1)}, u32[]{:S(2)}, u32[]{:S(2)}) %collective-permute-start.2) | collective-permute-done | bytes 98336 | tf_op jit(solution)/shard_map/ppermute | solution.py:69
  17.5 2.3 %collective-permute-done.3.refs_2_ = bf16[2,16,1536]{2,1,0:T(8,128)(2,1)S(1)} collective-permute-done((bf16[2,16,1536]{2,1,0:T(8,128)(2,1)}, bf16[2,16,1536]{2,1,0:T(8,128)(2,1)S(1)}, u32[]{:S(2)}, u32[]{:S(2)}) %collective-permute-start.3) | collective-permute-done | bytes 98336 | tf_op jit(solution)/shard_map/ppermute | solution.py:69
  23.2 6.5 %shard_map.168.refs_0_ = bf16[4,48,384]{2,1,0:T(8,128)(2,1)} custom-call(s32[4]{0:T(128)} %lengths_ref.1, s32[1,24]{1,0:T(1,128)} %slots_ref.1, bf16[48,1536]{1,0:T(8,128)(2,1)} %bitcast.63, bf16[2,512,1536]{2,1,0:T(8,128)(2,1)} %bitcast.60, bf16[2,192,1536]{2,1,0:T(8,128)(2,1)} %bitcast.61, bf16[2,16,1536]{2,1,0:T(8,128)(2,1)} %shard_map.167.refs_0_, ...), custom_call_target="tpu_custom_call" | custom-call | tf_op jit(solution)/shard_map/pallas_call | solution.py:218
  33.7 6.0 %collective-permute-done.5.refs_1_ = bf16[4,48,384]{2,1,0:T(8,128)(2,1)S(1)} collective-permute-done((bf16[4,48,384]{2,1,0:T(8,128)(2,1)S(1)}, bf16[4,48,384]{2,1,0:T(8,128)(2,1)S(1)}, u32[]{:S(2)}, u32[]{:S(2)}) %collective-permute-start.5) | collective-permute-done | bytes 147488 | tf_op jit(solution)/shard_map/ppermute | solution.py:76
  39.9 3.3 %constant_dynamic-slice_fusion.7 = (bf16[768,768]{1,0:T(8,128)(2,1)}, bf16[768,768]{1,0:T(8,128)(2,1)}) fusion(bf16[768,3072]{1,0:T(8,128)(2,1)} %param.26, s32[]{:T(128)S(6)} %select_n.124, s32[]{:T(128)S(6)} %select_n.123), kind=kLoop, calls=%fused_computation.53 | loop fusion | bytes 4718600 | tf_op jit(solution)/shard_map/dynamic_slice | solution.py:84
  43.2 2.5 %collective-permute-done.6.refs_2_ = bf16[4,48,384]{2,1,0:T(8,128)(2,1)S(1)} collective-permute-done((bf16[4,48,384]{2,1,0:T(8,128)(2,1)S(1)}, bf16[4,48,384]{2,1,0:T(8,128)(2,1)S(1)}, u32[]{:S(2)}, u32[]{:S(2)}) %collective-permute-start.6) | collective-permute-done | bytes 147488 | tf_op jit(solution)/shard_map/ppermute | solution.py:76
  45.7 1.8 %collective-permute-done.7.refs_3_ = bf16[4,48,384]{2,1,0:T(8,128)(2,1)S(1)} collective-permute-done((bf16[4,48,384]{2,1,0:T(8,128)(2,1)S(1)}, bf16[4,48,384]{2,1,0:T(8,128)(2,1)S(1)}, u32[]{:S(2)}, u32[]{:S(2)}) %collective-permute-start.7) | collective-permute-done | bytes 147488 | tf_op jit(solution)/shard_map/ppermute | solution.py:76
  48.1 3.7 %shard_map.169.refs_0_ = bf16[4,48,768]{2,1,0:T(8,128)(2,1)} custom-call(bf16[4,48,384]{2,1,0:T(8,128)(2,1)} %shard_map.168.refs_0_, bf16[4,48,384]{2,1,0:T(8,128)(2,1)} %copy-done.9, bf16[4,48,384]{2,1,0:T(8,128)(2,1)} %copy-done.10, bf16[4,48,384]{2,1,0:T(8,128)(2,1)} %copy-done.11, bf16[384,768]{1,0:T(8,128)(2,1)} %refs_4_.3, bf16[384,384]{1,0:T(8,128)(2,1)} %copy-done.4, ...), custom_call_target="tpu_custom_call" | custom-call | tf_op jit(solution)/shard_map/pallas_call | solution.py:272
  54.2 2.0 %collective-permute-start.12 = (bf16[4,48,768]{2,1,0:T(8,128)(2,1)}, bf16[4,48,768]{2,1,0:T(8,128)(2,1)S(1)}, u32[]{:S(2)}, u32[]{:S(2)}) collective-permute-start(bf16[4,48,768]{2,1,0:T(8,128)(2,1)} %shard_map.169.refs_0_), channel_id=1, source_target_pairs={{0,8},{4,12},{8,0},{12,4},{1,9},{5,13},{9,1},{13,5},{2,10},{6,14},... | collective-permute-start | bytes 884744 | tf_op jit(solution)/shard_map/ppermute | solution.py:76
  57.3 6.1 %collective-permute-done.11.refs_1_ = bf16[4,48,768]{2,1,0:T(8,128)(2,1)S(1)} collective-permute-done((bf16[4,48,768]{2,1,0:T(8,128)(2,1)}, bf16[4,48,768]{2,1,0:T(8,128)(2,1)S(1)}, u32[]{:S(2)}, u32[]{:S(2)}) %collective-permute-start.11) | collective-permute-done | bytes 294944 | tf_op jit(solution)/shard_map/ppermute | solution.py:76
  63.4 12.5 %collective-permute-start.14 = (bf16[4,48,768]{2,1,0:T(8,128)(2,1)}, bf16[4,48,768]{2,1,0:T(8,128)(2,1)S(1)}, u32[]{:S(2)}, u32[]{:S(2)}) collective-permute-start(bf16[4,48,768]{2,1,0:T(8,128)(2,1)} %shard_map.169.refs_0_), channel_id=1, source_target_pairs={{0,1},{1,0},{2,3},{3,2},{4,5},{5,4},{6,7},{7,6},{8,9},{9,8},{10,11... | collective-permute-start | bytes 884744 | tf_op jit(solution)/shard_map/ppermute | solution.py:49
  75.9 3.2 %constant_dynamic-slice_fusion.6 = bf16[1536,768]{1,0:T(8,128)(2,1)} fusion(bf16[3072,768]{1,0:T(8,128)(2,1)} %refs_2_.3, s32[]{:T(128)S(6)} %select_n.125), kind=kLoop, calls=%fused_computation.52 | loop fusion | bytes 4718596 | tf_op jit(solution)/shard_map/dynamic_slice | solution.py:84
  80.5 2.5 %collective-permute-done.13.refs_3_ = bf16[4,48,768]{2,1,0:T(8,128)(2,1)} collective-permute-done((bf16[4,48,768]{2,1,0:T(8,128)(2,1)}, bf16[4,48,768]{2,1,0:T(8,128)(2,1)}, u32[]{:S(2)}, u32[]{:S(2)}) %collective-permute-start.13) | collective-permute-done | bytes 294944 | tf_op jit(solution)/shard_map/ppermute | solution.py:76
  87.9 7.5 %shard_map.170 = (bf16[2,192,768]{2,1,0:T(8,128)(2,1)}, bf16[48,3072]{1,0:T(8,128)(2,1)}) custom-call(bf16[4,48,768]{2,1,0:T(8,128)(2,1)} %shard_map.169.refs_0_, bf16[4,48,768]{2,1,0:T(8,128)(2,1)} %copy-done.21, bf16[4,48,768]{2,1,0:T(8,128)(2,1)} %copy-done.23, bf16[4,48,768]{2,1,0:T(8,128)(2,1)} %collective-permute-done.13.refs_3_, ...), custom_call_target="tpu_custom_call" | custom-call | flops 3623878656 | bytes 18874368 | tf_op jit(solution)/shard_map/pallas_call | solution.py:357
  96.8 3.6 %collective-permute-done.21.refs_2_ = bf16[4,48,768]{2,1,0:T(8,128)(2,1)} collective-permute-done((bf16[4,48,768]{2,1,0:T(8,128)(2,1)S(1)}, bf16[4,48,768]{2,1,0:T(8,128)(2,1)}, u32[]{:S(2)}, u32[]{:S(2)}) %collective-permute-start.21) | collective-permute-done | bytes 294944 | tf_op jit(solution)/shard_map/ppermute | solution.py:49
  100.4 6.3 %collective-permute-done.22.refs_3_ = bf16[4,48,768]{2,1,0:T(8,128)(2,1)} collective-permute-done((bf16[4,48,768]{2,1,0:T(8,128)(2,1)}, bf16[4,48,768]{2,1,0:T(8,128)(2,1)}, u32[]{:S(2)}, u32[]{:S(2)}) %collective-permute-start.22) | collective-permute-done | bytes 294944 | tf_op jit(solution)/shard_map/ppermute | solution.py:49
  106.7 7.5 %shard_map.171 = (bf16[2,192,768]{2,1,0:T(8,128)(2,1)}, bf16[48,3072]{1,0:T(8,128)(2,1)}) custom-call(bf16[4,48,768]{2,1,0:T(8,128)(2,1)} %copy-done.22, bf16[4,48,768]{2,1,0:T(8,128)(2,1)} %collective-permute-done.20.refs_1_, bf16[4,48,768]{2,1,0:T(8,128)(2,1)} %collective-permute-done.21.refs_2_, bf16[4,48,768]{2,1,0:T(8,128)(2,1)} %collective-permute-done.22.refs_3_, ...), custom_call_target="tpu_custom_call" | custom-call | flops 3623878656 | bytes 18874368 | tf_op jit(solution)/shard_map/pallas_call | solution.py:357
  115.6 3.6 %collective-permute-done.24.refs_1_.refs_3_ = bf16[2,192,768]{2,1,0:T(8,128)(2,1)S(1)} collective-permute-done((bf16[2,192,768]{2,1,0:T(8,128)(2,1)}, bf16[2,192,768]{2,1,0:T(8,128)(2,1)S(1)}, u32[]{:S(2)}, u32[]{:S(2)}) %collective-permute-start.24) | collective-permute-done | bytes 589856 | tf_op jit(solution)/shard_map/ppermute | solution.py:49
  120.1 5.3 %shard_map.172 = (bf16[1,48,768]{2,1,0:T(8,128)(2,1)}, bf16[1,48,768]{2,1,0:T(8,128)(2,1)}, bf16[1,48,768]{2,1,0:T(8,128)(2,1)}, bf16[1,48,768]{2,1,0:T(8,128)(2,1)}) custom-call(bf16[2,192,768]{2,1,0:T(8,128)(2,1)} %get-tuple-element.105.refs_0_.refs_2_, bf16[2,192,768]{2,1,0:T(8,128)(2,1)} %copy-done.1, bf16[3072,768]{1,0:T(8,128)(2,1)} %refs_2_.3), custom_call_target="tpu_custom_call" | custom-call | flops 905969664 | bytes 4718592 | tf_op jit(solution)/shard_map/pallas_call | solution.py:423
  125.4 5.3 %collective-permute-done.23.refs_1_ = bf16[2,192,768]{2,1,0:T(8,128)(2,1)S(1)} collective-permute-done((bf16[2,192,768]{2,1,0:T(8,128)(2,1)}, bf16[2,192,768]{2,1,0:T(8,128)(2,1)S(1)}, u32[]{:S(2)}, u32[]{:S(2)}) %collective-permute-start.23) | collective-permute-done | bytes 589856 | tf_op jit(solution)/shard_map/ppermute | solution.py:49
  131.6 5.5 %shard_map.173 = (bf16[2,48,768]{2,1,0:T(8,128)(2,1)}, bf16[2,48,768]{2,1,0:T(8,128)(2,1)}, bf16[2,48,768]{2,1,0:T(8,128)(2,1)}, bf16[2,48,768]{2,1,0:T(8,128)(2,1)}) custom-call(bf16[2,192,768]{2,1,0:T(8,128)(2,1)} %get-tuple-element.100.refs_0_, bf16[2,192,768]{2,1,0:T(8,128)(2,1)} %copy-done.2, bf16[3072,768]{1,0:T(8,128)(2,1)} %refs_2_.3, ...), custom_call_target="tpu_custom_call" | custom-call | flops 905969664 | bytes 4718592 | tf_op jit(solution)/shard_map/pallas_call | solution.py:423
  139.0 1.9 %collective-permute-start.27 = (bf16[2,48,768]{2,1,0:T(8,128)(2,1)}, bf16[2,48,768]{2,1,0:T(8,128)(2,1)S(1)}, u32[]{:S(2)}, u32[]{:S(2)}) collective-permute-start(bf16[2,48,768]{2,1,0:T(8,128)(2,1)} %get-tuple-element.118), channel_id=1, source_target_pairs={{0,12},{4,0},{8,4},{12,8},{1,13},{5,1},{9,5},{13,9},{2,14},{6,2},{... | collective-permute-start | bytes 442376 | tf_op jit(solution)/shard_map/ppermute | solution.py:76
  143.3 6.9 %shard_map.174 = (bf16[2,48,768]{2,1,0:T(8,128)(2,1)}, bf16[2,48,768]{2,1,0:T(8,128)(2,1)}, bf16[2,48,768]{2,1,0:T(8,128)(2,1)}, bf16[2,48,768]{2,1,0:T(8,128)(2,1)}) custom-call(bf16[2,192,768]{2,1,0:T(8,128)(2,1)} %get-tuple-element.100.refs_0_, bf16[2,192,768]{2,1,0:T(8,128)(2,1)} %copy-done.2, bf16[2,192,768]{2,1,0:T(8,128)(2,1)} %get-tuple-element.105.refs_0_.refs_2_, ...), custom_call_target="tpu_custom_call" | custom-call | flops 1811939328 | bytes 4718592 | tf_op jit(solution)/shard_map/pallas_call | solution.py:423
  150.7 3.0 %collective-permute-start.31 = (bf16[2,48,768]{2,1,0:T(8,128)(2,1)}, bf16[2,48,768]{2,1,0:T(8,128)(2,1)S(1)}, u32[]{:S(2)}, u32[]{:S(2)}) collective-permute-start(bf16[2,48,768]{2,1,0:T(8,128)(2,1)} %get-tuple-element.123), channel_id=1, source_target_pairs={{0,8},{4,12},{8,0},{12,4},{1,9},{5,13},{9,1},{13,5},{2,10},{6,14},... | collective-permute-start | bytes 442376 | tf_op jit(solution)/shard_map/ppermute | solution.py:76
  154.1 3.1 %collective-permute-done.30 = bf16[2,48,768]{2,1,0:T(8,128)(2,1)S(1)} collective-permute-done((bf16[2,48,768]{2,1,0:T(8,128)(2,1)}, bf16[2,48,768]{2,1,0:T(8,128)(2,1)S(1)}, u32[]{:S(2)}, u32[]{:S(2)}) %collective-permute-start.30) | collective-permute-done | bytes 147488 | tf_op jit(solution)/shard_map/ppermute | solution.py:76
  157.3 7.4 %collective-permute-done.31 = bf16[2,48,768]{2,1,0:T(8,128)(2,1)S(1)} collective-permute-done((bf16[2,48,768]{2,1,0:T(8,128)(2,1)}, bf16[2,48,768]{2,1,0:T(8,128)(2,1)S(1)}, u32[]{:S(2)}, u32[]{:S(2)}) %collective-permute-start.31) | collective-permute-done | bytes 147488 | tf_op jit(solution)/shard_map/ppermute | solution.py:76
  164.6 2.8 %collective-permute-done.32 = bf16[2,48,768]{2,1,0:T(8,128)(2,1)S(1)} collective-permute-done((bf16[2,48,768]{2,1,0:T(8,128)(2,1)}, bf16[2,48,768]{2,1,0:T(8,128)(2,1)S(1)}, u32[]{:S(2)}, u32[]{:S(2)}) %collective-permute-start.32) | collective-permute-done | bytes 147488 | tf_op jit(solution)/shard_map/ppermute | solution.py:76
  169.0 1.7 collective-permute-start.34
  172.5 1.9 %collective-permute-done.35 = f32[24,64]{1,0:T(8,128)S(1)} collective-permute-done((f32[24,64]{1,0:T(8,128)S(1)}, f32[24,64]{1,0:T(8,128)S(1)}, u32[]{:S(2)}, u32[]{:S(2)}) %collective-permute-start.35) | collective-permute-done | bytes 6176 | tf_op jit(solution)/shard_map/ppermute | solution.py:619
  (116 shorter events, 38.4 us)
Async XLA Ops:
  5.4 14.4 %collective-permute-start = (bf16[384,384]{1,0:T(8,128)(2,1)}, bf16[384,384]{1,0:T(8,128)(2,1)S(1)}, u32[]{:S(2)}, u32[]{:S(2)}) collective-permute-start(bf16[384,384]{1,0:T(8,128)(2,1)} %constant_dynamic-slice_fusion.9), channel_id=1, source_target_pairs={{0,1},{1,0},{2,3},{3,2},{4,5},{5,4},{6,7},{7,6},{8,9},{9,8},{10,11... | collective-permute-start | bytes 884744 | tf_op jit(solution)/shard_map/ppermute | solution.py:49
  6.9 12.9 %collective-permute-start.1 = (bf16[384,384]{1,0:T(8,128)(2,1)}, bf16[384,384]{1,0:T(8,128)(2,1)S(1)}, u32[]{:S(2)}, u32[]{:S(2)}) collective-permute-start(bf16[384,384]{1,0:T(8,128)(2,1)} %constant_dynamic-slice_fusion.9), channel_id=1, source_target_pairs={{0,2},{1,3},{2,0},{3,1},{4,6},{5,7},{6,4},{7,5},{8,10},{9,11},{10,... | collective-permute-start | bytes 884744 | tf_op jit(solution)/shard_map/ppermute | solution.py:57
  8.4 9.1 %collective-permute-start.2 = (bf16[2,16,1536]{2,1,0:T(8,128)(2,1)}, bf16[2,16,1536]{2,1,0:T(8,128)(2,1)S(1)}, u32[]{:S(2)}, u32[]{:S(2)}) collective-permute-start(bf16[2,16,1536]{2,1,0:T(8,128)(2,1)} %shard_map.167.refs_0_), channel_id=1, source_target_pairs={{0,1},{1,0},{2,3},{3,2},{4,5},{5,4},{6,7},{7,6},{8,9},{9,8},{10,11... | collective-permute-start | bytes 294920 | tf_op jit(solution)/shard_map/ppermute | solution.py:69
  8.9 10.8 %collective-permute-start.3 = (bf16[2,16,1536]{2,1,0:T(8,128)(2,1)}, bf16[2,16,1536]{2,1,0:T(8,128)(2,1)S(1)}, u32[]{:S(2)}, u32[]{:S(2)}) collective-permute-start(bf16[2,16,1536]{2,1,0:T(8,128)(2,1)} %shard_map.167.refs_0_), channel_id=1, source_target_pairs={{0,2},{1,3},{2,0},{3,1},{4,6},{5,7},{6,4},{7,5},{8,10},{9,11},{10,... | collective-permute-start | bytes 294920 | tf_op jit(solution)/shard_map/ppermute | solution.py:69
  9.4 10.3 %collective-permute-start.4 = (bf16[2,16,1536]{2,1,0:T(8,128)(2,1)}, bf16[2,16,1536]{2,1,0:T(8,128)(2,1)}, u32[]{:S(2)}, u32[]{:S(2)}) collective-permute-start(bf16[2,16,1536]{2,1,0:T(8,128)(2,1)} %shard_map.167.refs_0_), channel_id=1, source_target_pairs={{0,3},{1,2},{2,1},{3,0},{4,7},{5,6},{6,5},{7,4},{8,11},{9,10},{10,... | collective-permute-start | bytes 294920 | tf_op jit(solution)/shard_map/ppermute | solution.py:69
  19.8 10.0 %collective-permute-start.8 = (bf16[384,384]{1,0:T(8,128)(2,1)S(1)}, bf16[384,384]{1,0:T(8,128)(2,1)S(1)}, u32[]{:S(2)}, u32[]{:S(2)}) collective-permute-start(bf16[384,384]{1,0:T(8,128)(2,1)S(1)} %collective-permute-done.refs_5_), channel_id=1, source_target_pairs={{0,2},{1,3},{2,0},{3,1},{4,6},{5,7},{6,4},{7,5},{8,10},{9,11},{10,... | collective-permute-start | bytes 884744 | tf_op jit(solution)/shard_map/ppermute | solution.py:57
  21.4 26.1 %collective-permute-start.10 = (bf16[768,768]{1,0:T(8,128)(2,1)S(1)}, bf16[768,768]{1,0:T(8,128)(2,1)}, u32[]{:S(2)}, u32[]{:S(2)}) collective-permute-start(bf16[768,768]{1,0:T(8,128)(2,1)S(1)} %get-tuple-element.78), channel_id=1, source_target_pairs={{0,1},{1,0},{2,3},{3,2},{4,5},{5,4},{6,7},{7,6},{8,9},{9,8},{10,11... | collective-permute-start | bytes 3538952 | tf_op jit(solution)/shard_map/ppermute | solution.py:49
  21.9 31.4 %collective-permute-start.15 = (bf16[768,768]{1,0:T(8,128)(2,1)S(1)}, bf16[768,768]{1,0:T(8,128)(2,1)}, u32[]{:S(2)}, u32[]{:S(2)}) collective-permute-start(bf16[768,768]{1,0:T(8,128)(2,1)S(1)} %get-tuple-element.77), channel_id=1, source_target_pairs={{0,2},{1,3},{2,0},{3,1},{4,6},{5,7},{6,4},{7,5},{8,10},{9,11},{10,... | collective-permute-start | bytes 3538952 | tf_op jit(solution)/shard_map/ppermute | solution.py:57
  30.8 16.6 %collective-permute-start.9 = (bf16[1152,384]{1,0:T(8,128)(2,1)}, bf16[1152,384]{1,0:T(8,128)(2,1)}, u32[]{:S(2)}, u32[]{:S(2)}) collective-permute-start(bf16[1152,384]{1,0:T(8,128)(2,1)} %pad_maximum_fusion), channel_id=1, source_target_pairs={{0,16},{16,0},{1,17},{17,1},{2,18},{18,2},{3,19},{19,3},{4,20},{20... | collective-permute-start | bytes 2654216 | tf_op jit(solution)/shard_map/ppermute | solution.py:80
  30.9 8.8 %collective-permute-start.5 = (bf16[4,48,384]{2,1,0:T(8,128)(2,1)S(1)}, bf16[4,48,384]{2,1,0:T(8,128)(2,1)S(1)}, u32[]{:S(2)}, u32[]{:S(2)}) collective-permute-start(bf16[4,48,384]{2,1,0:T(8,128)(2,1)S(1)} %copy-done.8), channel_id=1, source_target_pairs={{0,4},{4,8},{8,12},{12,0},{1,5},{5,9},{9,13},{13,1},{2,6},{6,10},{... | collective-permute-start | bytes 442376 | tf_op jit(solution)/shard_map/ppermute | solution.py:76
  32.5 13.2 %collective-permute-start.6 = (bf16[4,48,384]{2,1,0:T(8,128)(2,1)S(1)}, bf16[4,48,384]{2,1,0:T(8,128)(2,1)S(1)}, u32[]{:S(2)}, u32[]{:S(2)}) collective-permute-start(bf16[4,48,384]{2,1,0:T(8,128)(2,1)S(1)} %copy-done.8), channel_id=1, source_target_pairs={{0,8},{4,12},{8,0},{12,4},{1,9},{5,13},{9,1},{13,5},{2,10},{6,14},... | collective-permute-start | bytes 442376 | tf_op jit(solution)/shard_map/ppermute | solution.py:76
  39.7 7.8 %collective-permute-start.7 = (bf16[4,48,384]{2,1,0:T(8,128)(2,1)S(1)}, bf16[4,48,384]{2,1,0:T(8,128)(2,1)S(1)}, u32[]{:S(2)}, u32[]{:S(2)}) collective-permute-start(bf16[4,48,384]{2,1,0:T(8,128)(2,1)S(1)} %copy-done.8), channel_id=1, source_target_pairs={{0,12},{4,0},{8,4},{12,8},{1,13},{5,1},{9,5},{13,9},{2,14},{6,2},{... | collective-permute-start | bytes 442376 | tf_op jit(solution)/shard_map/ppermute | solution.py:76
  51.8 31.1 %collective-permute-start.17 = (bf16[768,768]{1,0:T(8,128)(2,1)}, bf16[768,768]{1,0:T(8,128)(2,1)S(1)}, u32[]{:S(2)}, u32[]{:S(2)}) collective-permute-start(bf16[768,768]{1,0:T(8,128)(2,1)} %collective-permute-done.10.refs_7_), channel_id=1, source_target_pairs={{0,2},{1,3},{2,0},{3,1},{4,6},{5,7},{6,4},{7,5},{8,10},{9,11},{10,... | collective-permute-start | bytes 3538952 | tf_op jit(solution)/shard_map/ppermute | solution.py:57
  53.4 29.6 %collective-permute-start.16 = (bf16[768,768]{1,0:T(8,128)(2,1)}, bf16[768,768]{1,0:T(8,128)(2,1)S(1)}, u32[]{:S(2)}, u32[]{:S(2)}) collective-permute-start(bf16[768,768]{1,0:T(8,128)(2,1)} %collective-permute-done.15.refs_9_), channel_id=1, source_target_pairs={{0,16},{16,0},{1,17},{17,1},{2,18},{18,2},{3,19},{19,3},{4,20},{20... | collective-permute-start | bytes 3538952 | tf_op jit(solution)/shard_map/ppermute | solution.py:80
  53.4 10.0 %collective-permute-start.11 = (bf16[4,48,768]{2,1,0:T(8,128)(2,1)}, bf16[4,48,768]{2,1,0:T(8,128)(2,1)S(1)}, u32[]{:S(2)}, u32[]{:S(2)}) collective-permute-start(bf16[4,48,768]{2,1,0:T(8,128)(2,1)} %shard_map.169.refs_0_), channel_id=1, source_target_pairs={{0,4},{4,8},{8,12},{12,0},{1,5},{5,9},{9,13},{13,1},{2,6},{6,10},{... | collective-permute-start | bytes 884744 | tf_op jit(solution)/shard_map/ppermute | solution.py:76
  54.2 26.2 %collective-permute-start.12 = (bf16[4,48,768]{2,1,0:T(8,128)(2,1)}, bf16[4,48,768]{2,1,0:T(8,128)(2,1)S(1)}, u32[]{:S(2)}, u32[]{:S(2)}) collective-permute-start(bf16[4,48,768]{2,1,0:T(8,128)(2,1)} %shard_map.169.refs_0_), channel_id=1, source_target_pairs={{0,8},{4,12},{8,0},{12,4},{1,9},{5,13},{9,1},{13,5},{2,10},{6,14},... | collective-permute-start | bytes 884744 | tf_op jit(solution)/shard_map/ppermute | solution.py:76
  56.3 26.7 %collective-permute-start.13 = (bf16[4,48,768]{2,1,0:T(8,128)(2,1)}, bf16[4,48,768]{2,1,0:T(8,128)(2,1)}, u32[]{:S(2)}, u32[]{:S(2)}) collective-permute-start(bf16[4,48,768]{2,1,0:T(8,128)(2,1)} %shard_map.169.refs_0_), channel_id=1, source_target_pairs={{0,12},{4,0},{8,4},{12,8},{1,13},{5,1},{9,5},{13,9},{2,14},{6,2},{... | collective-permute-start | bytes 884744 | tf_op jit(solution)/shard_map/ppermute | solution.py:76
  63.4 19.6 %collective-permute-start.14 = (bf16[4,48,768]{2,1,0:T(8,128)(2,1)}, bf16[4,48,768]{2,1,0:T(8,128)(2,1)S(1)}, u32[]{:S(2)}, u32[]{:S(2)}) collective-permute-start(bf16[4,48,768]{2,1,0:T(8,128)(2,1)} %shard_map.169.refs_0_), channel_id=1, source_target_pairs={{0,1},{1,0},{2,3},{3,2},{4,5},{5,4},{6,7},{7,6},{8,9},{9,8},{10,11... | collective-permute-start | bytes 884744 | tf_op jit(solution)/shard_map/ppermute | solution.py:49
  83.1 4.8 %collective-permute-start.19 = (bf16[768,768]{1,0:T(8,128)(2,1)S(1)}, bf16[768,768]{1,0:T(8,128)(2,1)}, u32[]{:S(2)}, u32[]{:S(2)}) collective-permute-start(bf16[768,768]{1,0:T(8,128)(2,1)S(1)} %collective-permute-done.17.refs_11_), channel_id=1, source_target_pairs={{0,16},{16,0},{1,17},{17,1},{2,18},{18,2},{3,19},{19,3},{4,20},{20... | collective-permute-start | bytes 3538952 | tf_op jit(solution)/shard_map/ppermute | solution.py:80
  83.6 53.5 %collective-permute-start.28 = (bf16[1536,768]{1,0:T(8,128)(2,1)}, bf16[1536,768]{1,0:T(8,128)(2,1)}, u32[]{:S(2)}, u32[]{:S(2)}) collective-permute-start(bf16[1536,768]{1,0:T(8,128)(2,1)} %constant_dynamic-slice_fusion.6), channel_id=1, source_target_pairs={{0,2},{1,3},{2,0},{3,1},{4,6},{5,7},{6,4},{7,5},{8,10},{9,11},{10,... | collective-permute-start | bytes 7077896 | tf_op jit(solution)/shard_map/ppermute | solution.py:57
  84.1 12.7 %collective-permute-start.20 = (bf16[4,48,768]{2,1,0:T(8,128)(2,1)S(1)}, bf16[4,48,768]{2,1,0:T(8,128)(2,1)}, u32[]{:S(2)}, u32[]{:S(2)}) collective-permute-start(bf16[4,48,768]{2,1,0:T(8,128)(2,1)S(1)} %collective-permute-done.11.refs_1_), channel_id=1, source_target_pairs={{0,1},{1,0},{2,3},{3,2},{4,5},{5,4},{6,7},{7,6},{8,9},{9,8},{10,11... | collective-permute-start | bytes 884744 | tf_op jit(solution)/shard_map/ppermute | solution.py:49
  85.4 15.0 %collective-permute-start.21 = (bf16[4,48,768]{2,1,0:T(8,128)(2,1)S(1)}, bf16[4,48,768]{2,1,0:T(8,128)(2,1)}, u32[]{:S(2)}, u32[]{:S(2)}) collective-permute-start(bf16[4,48,768]{2,1,0:T(8,128)(2,1)S(1)} %collective-permute-done.12.refs_2_), channel_id=1, source_target_pairs={{0,1},{1,0},{2,3},{3,2},{4,5},{5,4},{6,7},{7,6},{8,9},{9,8},{10,11... | collective-permute-start | bytes 884744 | tf_op jit(solution)/shard_map/ppermute | solution.py:49
  87.2 19.6 %collective-permute-start.22 = (bf16[4,48,768]{2,1,0:T(8,128)(2,1)}, bf16[4,48,768]{2,1,0:T(8,128)(2,1)}, u32[]{:S(2)}, u32[]{:S(2)}) collective-permute-start(bf16[4,48,768]{2,1,0:T(8,128)(2,1)} %collective-permute-done.13.refs_3_), channel_id=1, source_target_pairs={{0,1},{1,0},{2,3},{3,2},{4,5},{5,4},{6,7},{7,6},{8,9},{9,8},{10,11... | collective-permute-start | bytes 884744 | tf_op jit(solution)/shard_map/ppermute | solution.py:49
  95.5 23.8 %collective-permute-start.24 = (bf16[2,192,768]{2,1,0:T(8,128)(2,1)}, bf16[2,192,768]{2,1,0:T(8,128)(2,1)S(1)}, u32[]{:S(2)}, u32[]{:S(2)}) collective-permute-start(bf16[2,192,768]{2,1,0:T(8,128)(2,1)} %get-tuple-element.100.refs_0_), channel_id=1, source_target_pairs={{0,1},{1,0},{2,3},{3,2},{4,5},{5,4},{6,7},{7,6},{8,9},{9,8},{10,11... | collective-permute-start | bytes 1769480 | tf_op jit(solution)/shard_map/ppermute | solution.py:49
  114.2 16.5 %collective-permute-start.23 = (bf16[2,192,768]{2,1,0:T(8,128)(2,1)}, bf16[2,192,768]{2,1,0:T(8,128)(2,1)S(1)}, u32[]{:S(2)}, u32[]{:S(2)}) collective-permute-start(bf16[2,192,768]{2,1,0:T(8,128)(2,1)} %get-tuple-element.105.refs_0_.refs_2_), channel_id=1, source_target_pairs={{0,1},{1,0},{2,3},{3,2},{4,5},{5,4},{6,7},{7,6},{8,9},{9,8},{10,11... | collective-permute-start | bytes 1769480 | tf_op jit(solution)/shard_map/ppermute | solution.py:49
  137.1 4.8 %collective-permute-start.29 = (bf16[1536,768]{1,0:T(8,128)(2,1)}, bf16[1536,768]{1,0:T(8,128)(2,1)S(1)}, u32[]{:S(2)}, u32[]{:S(2)}) collective-permute-start(bf16[1536,768]{1,0:T(8,128)(2,1)} %collective-permute-done.28.refs_4_), channel_id=1, source_target_pairs={{0,16},{16,0},{1,17},{17,1},{2,18},{18,2},{3,19},{19,3},{4,20},{20... | collective-permute-start | bytes 7077896 | tf_op jit(solution)/shard_map/ppermute | solution.py:80
  138.1 15.6 %collective-permute-start.25 = (bf16[2,48,768]{2,1,0:T(8,128)(2,1)}, bf16[2,48,768]{2,1,0:T(8,128)(2,1)S(1)}, u32[]{:S(2)}, u32[]{:S(2)}) collective-permute-start(bf16[2,48,768]{2,1,0:T(8,128)(2,1)} %get-tuple-element.116), channel_id=1, source_target_pairs={{0,4},{4,8},{8,12},{12,0},{1,5},{5,9},{9,13},{13,1},{2,6},{6,10},{... | collective-permute-start | bytes 442376 | tf_op jit(solution)/shard_map/ppermute | solution.py:76
  138.5 15.2 %collective-permute-start.26 = (bf16[2,48,768]{2,1,0:T(8,128)(2,1)}, bf16[2,48,768]{2,1,0:T(8,128)(2,1)S(1)}, u32[]{:S(2)}, u32[]{:S(2)}) collective-permute-start(bf16[2,48,768]{2,1,0:T(8,128)(2,1)} %get-tuple-element.117), channel_id=1, source_target_pairs={{0,8},{4,12},{8,0},{12,4},{1,9},{5,13},{9,1},{13,5},{2,10},{6,14},... | collective-permute-start | bytes 442376 | tf_op jit(solution)/shard_map/ppermute | solution.py:76
  139.0 14.7 %collective-permute-start.27 = (bf16[2,48,768]{2,1,0:T(8,128)(2,1)}, bf16[2,48,768]{2,1,0:T(8,128)(2,1)S(1)}, u32[]{:S(2)}, u32[]{:S(2)}) collective-permute-start(bf16[2,48,768]{2,1,0:T(8,128)(2,1)} %get-tuple-element.118), channel_id=1, source_target_pairs={{0,12},{4,0},{8,4},{12,8},{1,13},{5,1},{9,5},{13,9},{2,14},{6,2},{... | collective-permute-start | bytes 442376 | tf_op jit(solution)/shard_map/ppermute | solution.py:76
  150.3 7.0 %collective-permute-start.30 = (bf16[2,48,768]{2,1,0:T(8,128)(2,1)}, bf16[2,48,768]{2,1,0:T(8,128)(2,1)S(1)}, u32[]{:S(2)}, u32[]{:S(2)}) collective-permute-start(bf16[2,48,768]{2,1,0:T(8,128)(2,1)} %get-tuple-element.122), channel_id=1, source_target_pairs={{0,4},{4,8},{8,12},{12,0},{1,5},{5,9},{9,13},{13,1},{2,6},{6,10},{... | collective-permute-start | bytes 442376 | tf_op jit(solution)/shard_map/ppermute | solution.py:76
  150.7 13.9 %collective-permute-start.31 = (bf16[2,48,768]{2,1,0:T(8,128)(2,1)}, bf16[2,48,768]{2,1,0:T(8,128)(2,1)S(1)}, u32[]{:S(2)}, u32[]{:S(2)}) collective-permute-start(bf16[2,48,768]{2,1,0:T(8,128)(2,1)} %get-tuple-element.123), channel_id=1, source_target_pairs={{0,8},{4,12},{8,0},{12,4},{1,9},{5,13},{9,1},{13,5},{2,10},{6,14},... | collective-permute-start | bytes 442376 | tf_op jit(solution)/shard_map/ppermute | solution.py:76
  153.7 13.8 %collective-permute-start.32 = (bf16[2,48,768]{2,1,0:T(8,128)(2,1)}, bf16[2,48,768]{2,1,0:T(8,128)(2,1)S(1)}, u32[]{:S(2)}, u32[]{:S(2)}) collective-permute-start(bf16[2,48,768]{2,1,0:T(8,128)(2,1)} %get-tuple-element.124), channel_id=1, source_target_pairs={{0,12},{4,0},{8,4},{12,8},{1,13},{5,1},{9,5},{13,9},{2,14},{6,2},{... | collective-permute-start | bytes 442376 | tf_op jit(solution)/shard_map/ppermute | solution.py:76
  (28 other events, 342.0 us)

commit v2 on v1

--- a/solution.py
+++ b/solution.py
@@ -530,26 +530,26 @@
         modulation,
     )
     along_z = [send_z(residual, dz) for dz in range(requests)]
-    near = [send_x(residual, dx) for dx in range(wide)]
+    along_z[0] = residual
+    near = [[send_x(block, dx) for block in along_z[:2]] for dx in range(1, wide)]
 
     up_x[1:], _ = lax.optimization_barrier((up_x[1:], residual))
-    other_y = [swap_core(part) for part in up_y[1:]]
     up_mine = [send_y(up_x[dx], dy) if dx else up_y[dy] for dy, dx in around]
 
     down_cols = down_weight.shape[1]
     down_half = hidden // 2
     own_down = take(down_weight, cfg_id * down_half, down_half, 0)
-    along_z, near, other_y, up_mine, own_down = lax.optimization_barrier(
-        (along_z, near, other_y, up_mine, own_down)
+    along_z, near, up_mine, own_down = lax.optimization_barrier(
+        (along_z, near, up_mine, own_down)
     )
-    blocks = [
-        [send_x(block, dx) if dz else near[dx] for dz, block in enumerate(along_z)]
-        for dx in range(wide)
+    blocks = [along_z]
+    blocks += [
+        near[dx - 1] + [send_x(block, dx) for block in along_z[2:]] for dx in range(1, wide)
     ]
     down_mine = [send_y(own_down, dy) for dy in range(1, high)]
     up_pieces = [("halves", own_up)]
     for part, (dy, dx) in zip(up_mine[1:], around[1:]):
-        up_pieces.append(("core", [part, swap_core(part) if dx else other_y[dy - 1]]))
+        up_pieces.append(("core", [part, swap_core(part)]))
 
     acts, own_rows = [], []
     for dx in range(wide):

time: 176 us -> 178 us (1.011)
  waiting for transfers between devices: 62.6 us -> 69.9 us
  starting transfers between devices: 46 us -> 40.8 us
    ppermute x5, waiting for transfers between devices: 0.17 us -> 13.2 us  [send_y(): return lax.ppermute(block, 'seq', route)]
    ppermute x8, starting transfers between devices: 20 us -> 9.38 us  [send_x(): return lax.ppermute(block, 'seq', route)]
    ppermute x8, waiting for transfers between devices: 18.9 us -> 13.8 us  [send_x(): return lax.ppermute(block, 'seq', route)]
    ppermute x12, starting transfers between devices: 13.3 us -> 18.2 us  [send_z(): lax.ppermute(block, 'req', [(r, (r + step) % count) for r in range(count)])]
    unnamed x49 -> x53, local copies, waits for them, and re-layouts: 5.23 us -> 4.8 us
  transfers between devices with their start and end apart: 36 -> 36, of which waited for: 20 -> 22; matrix products, arithmetic and copies ran while one was open for 6% -> 6% of each run, Pallas kernels for 24% -> 24%
where the time goes in v2:
time: 178 us; the launch traced here: 177 us
  waiting for transfers between devices  69.9 us (39%)
  Pallas kernels  44.5 us (25%)
  starting transfers between devices  40.8 us (23%)
  local copies, waits for them, and re-layouts  15.6 us (9%)
  other arithmetic  4.07 us (2%)
    ppermute x12, waiting for transfers between devices, send_z(): lax.ppermute(block, 'req', [(r, (r + step) % count) for r in range(count)])  32.7 us
    ppermute x12, starting transfers between devices, send_z(): lax.ppermute(block, 'req', [(r, (r + step) % count) for r in range(count)])  18.2 us
    pallas_call x3, Pallas kernels, down_products(): pl.pallas_call(functools.partial(down_kernel, requests, wide, blocks, len...  17.7 us
    pallas_call x2, Pallas kernels, up_products(): pl.pallas_call(functools.partial(up_kernel, requests, around, [kind for k...  15 us
    ppermute x8, waiting for transfers between devices, send_x(): return lax.ppermute(block, 'seq', route)  13.8 us
    ppermute x5, waiting for transfers between devices, send_y(): return lax.ppermute(block, 'seq', route)  13.2 us
    dynamic_slice x5, local copies, waits for them, and re-layouts, take(): return lax.dynamic_slice_in_dim(array, start, size, axis)  10.1 us
    ppermute x8, starting transfers between devices, send_x(): return lax.ppermute(block, 'seq', route)  9.38 us
  transfers between devices with their start and end apart: 36, of which 22 were waited for; matrix products, arithmetic and copies ran while one was open for 6% of the time, Pallas kernels for 24%

profile of v2, /device:TPU:8, one launch (start us, length us, event | category | flops | bytes accessed | tf_op | source)
XLA Modules:
  0.0 177.3 jit_solution(11729932759025745776)
XLA Ops:
  3.7 1.7 constant_dynamic-slice_fusion.9
  9.4 2.4 %collective-permute-start.4 = (bf16[2,16,1536]{2,1,0:T(8,128)(2,1)}, bf16[2,16,1536]{2,1,0:T(8,128)(2,1)}, u32[]{:S(2)}, u32[]{:S(2)}) collective-permute-start(bf16[2,16,1536]{2,1,0:T(8,128)(2,1)} %shard_map.167.refs_0_), channel_id=1, source_target_pairs={{0,3},{1,2},{2,1},{3,0},{4,7},{5,6},{6,5},{7,4},{8,11},{9,10},{10,... | collective-permute-start | bytes 294920 | tf_op jit(solution)/shard_map/ppermute | solution.py:69
  11.9 1.8 %constant_dynamic-slice_fusion.10 = (bf16[768,768]{1,0:T(8,128)(2,1)S(1)}, bf16[768,768]{1,0:T(8,128)(2,1)S(1)}) fusion(bf16[768,3072]{1,0:T(8,128)(2,1)} %param.26, s32[]{:T(128)S(6)} %select_n.121, s32[]{:T(128)S(6)} %select_n.119), kind=kLoop, calls=%fused_computation.56 | loop fusion | bytes 4718600 | tf_op jit(solution)/shard_map/dynamic_slice | solution.py:84
  13.7 3.8 %collective-permute-done.2.refs_1_ = bf16[2,16,1536]{2,1,0:T(8,128)(2,1)S(1)} collective-permute-done((bf16[2,16,1536]{2,1,0:T(8,128)(2,1)}, bf16[2,16,1536]{2,1,0:T(8,128)(2,1)S(1)}, u32[]{:S(2)}, u32[]{:S(2)}) %collective-permute-start.2) | collective-permute-done | bytes 98336 | tf_op jit(solution)/shard_map/ppermute | solution.py:69
  17.5 2.3 %collective-permute-done.3.refs_2_ = bf16[2,16,1536]{2,1,0:T(8,128)(2,1)S(1)} collective-permute-done((bf16[2,16,1536]{2,1,0:T(8,128)(2,1)}, bf16[2,16,1536]{2,1,0:T(8,128)(2,1)S(1)}, u32[]{:S(2)}, u32[]{:S(2)}) %collective-permute-start.3) | collective-permute-done | bytes 98336 | tf_op jit(solution)/shard_map/ppermute | solution.py:69
  21.9 6.5 %shard_map.168.refs_0_ = bf16[4,48,384]{2,1,0:T(8,128)(2,1)} custom-call(s32[4]{0:T(128)} %lengths_ref.1, s32[1,24]{1,0:T(1,128)} %slots_ref.1, bf16[48,1536]{1,0:T(8,128)(2,1)} %bitcast.63, bf16[2,512,1536]{2,1,0:T(8,128)(2,1)} %bitcast.60, bf16[2,192,1536]{2,1,0:T(8,128)(2,1)} %bitcast.61, bf16[2,16,1536]{2,1,0:T(8,128)(2,1)} %shard_map.167.refs_0_, ...), custom_call_target="tpu_custom_call" | custom-call | tf_op jit(solution)/shard_map/pallas_call | solution.py:218
  29.5 1.6 collective-permute-start.5
  33.6 2.1 %collective-permute-done.5.refs_1_ = bf16[4,48,384]{2,1,0:T(8,128)(2,1)S(1)} collective-permute-done((bf16[4,48,384]{2,1,0:T(8,128)(2,1)S(1)}, bf16[4,48,384]{2,1,0:T(8,128)(2,1)S(1)}, u32[]{:S(2)}, u32[]{:S(2)}) %collective-permute-start.5) | collective-permute-done | bytes 147488 | tf_op jit(solution)/shard_map/ppermute | solution.py:76
  35.7 2.8 %collective-permute-start.7 = (bf16[4,48,384]{2,1,0:T(8,128)(2,1)S(1)}, bf16[4,48,384]{2,1,0:T(8,128)(2,1)S(1)}, u32[]{:S(2)}, u32[]{:S(2)}) collective-permute-start(bf16[4,48,384]{2,1,0:T(8,128)(2,1)S(1)} %copy-done.8), channel_id=1, source_target_pairs={{0,12},{4,0},{8,4},{12,8},{1,13},{5,1},{9,5},{13,9},{2,14},{6,2},{... | collective-permute-start | bytes 442376 | tf_op jit(solution)/shard_map/ppermute | solution.py:76
  38.5 3.3 %constant_dynamic-slice_fusion.7 = (bf16[768,768]{1,0:T(8,128)(2,1)}, bf16[768,768]{1,0:T(8,128)(2,1)}) fusion(bf16[768,3072]{1,0:T(8,128)(2,1)} %param.26, s32[]{:T(128)S(6)} %select_n.124, s32[]{:T(128)S(6)} %select_n.123), kind=kLoop, calls=%fused_computation.53 | loop fusion | bytes 4718600 | tf_op jit(solution)/shard_map/dynamic_slice | solution.py:84
  41.8 2.5 %collective-permute-done.6.refs_2_ = bf16[4,48,384]{2,1,0:T(8,128)(2,1)S(1)} collective-permute-done((bf16[4,48,384]{2,1,0:T(8,128)(2,1)S(1)}, bf16[4,48,384]{2,1,0:T(8,128)(2,1)S(1)}, u32[]{:S(2)}, u32[]{:S(2)}) %collective-permute-start.6) | collective-permute-done | bytes 147488 | tf_op jit(solution)/shard_map/ppermute | solution.py:76
  44.3 1.8 %collective-permute-done.7.refs_3_ = bf16[4,48,384]{2,1,0:T(8,128)(2,1)S(1)} collective-permute-done((bf16[4,48,384]{2,1,0:T(8,128)(2,1)S(1)}, bf16[4,48,384]{2,1,0:T(8,128)(2,1)S(1)}, u32[]{:S(2)}, u32[]{:S(2)}) %collective-permute-start.7) | collective-permute-done | bytes 147488 | tf_op jit(solution)/shard_map/ppermute | solution.py:76
  46.8 3.7 %shard_map.169.refs_0_ = bf16[4,48,768]{2,1,0:T(8,128)(2,1)} custom-call(bf16[4,48,384]{2,1,0:T(8,128)(2,1)} %shard_map.168.refs_0_, bf16[4,48,384]{2,1,0:T(8,128)(2,1)} %copy-done.9, bf16[4,48,384]{2,1,0:T(8,128)(2,1)} %copy-done.10, bf16[4,48,384]{2,1,0:T(8,128)(2,1)} %copy-done.11, bf16[384,768]{1,0:T(8,128)(2,1)} %refs_4_.3, bf16[384,384]{1,0:T(8,128)(2,1)} %copy-done.4, ...), custom_call_target="tpu_custom_call" | custom-call | tf_op jit(solution)/shard_map/pallas_call | solution.py:272
  54.7 1.8 collective-permute-start.13
  56.4 3.6 %collective-permute-done.16.refs_9_ = bf16[768,768]{1,0:T(8,128)(2,1)} collective-permute-done((bf16[768,768]{1,0:T(8,128)(2,1)S(1)}, bf16[768,768]{1,0:T(8,128)(2,1)}, u32[]{:S(2)}, u32[]{:S(2)}) %collective-permute-start.16) | collective-permute-done | bytes 1179680 | tf_op jit(solution)/shard_map/ppermute | solution.py:57
  61.5 12.3 %collective-permute-done.11.refs_1_ = bf16[4,48,768]{2,1,0:T(8,128)(2,1)S(1)} collective-permute-done((bf16[4,48,768]{2,1,0:T(8,128)(2,1)}, bf16[4,48,768]{2,1,0:T(8,128)(2,1)S(1)}, u32[]{:S(2)}, u32[]{:S(2)}) %collective-permute-start.11) | collective-permute-done | bytes 294944 | tf_op jit(solution)/shard_map/ppermute | solution.py:76
  75.1 3.2 %constant_dynamic-slice_fusion.6 = bf16[1536,768]{1,0:T(8,128)(2,1)} fusion(bf16[3072,768]{1,0:T(8,128)(2,1)} %refs_2_.3, s32[]{:T(128)S(6)} %select_n.125), kind=kLoop, calls=%fused_computation.52 | loop fusion | bytes 4718596 | tf_op jit(solution)/shard_map/dynamic_slice | solution.py:84
  80.5 3.9 %collective-permute-done.17.refs_11_ = bf16[768,768]{1,0:T(8,128)(2,1)S(1)} collective-permute-done((bf16[768,768]{1,0:T(8,128)(2,1)}, bf16[768,768]{1,0:T(8,128)(2,1)S(1)}, u32[]{:S(2)}, u32[]{:S(2)}) %collective-permute-start.17) | collective-permute-done | bytes 1179680 | tf_op jit(solution)/shard_map/ppermute | solution.py:57
  86.9 2.2 %collective-permute-done.18.refs_8_ = bf16[768,768]{1,0:T(8,128)(2,1)S(1)} collective-permute-done((bf16[768,768]{1,0:T(8,128)(2,1)}, bf16[768,768]{1,0:T(8,128)(2,1)S(1)}, u32[]{:S(2)}, u32[]{:S(2)}) %collective-permute-start.18) | collective-permute-done | bytes 1179680 | tf_op jit(solution)/shard_map/ppermute | solution.py:80
  90.8 7.5 %shard_map.170 = (bf16[2,192,768]{2,1,0:T(8,128)(2,1)}, bf16[48,3072]{1,0:T(8,128)(2,1)}) custom-call(bf16[4,48,768]{2,1,0:T(8,128)(2,1)} %shard_map.169.refs_0_, bf16[4,48,768]{2,1,0:T(8,128)(2,1)} %copy-done.21, bf16[4,48,768]{2,1,0:T(8,128)(2,1)} %copy-done.23, bf16[4,48,768]{2,1,0:T(8,128)(2,1)} %collective-permute-done.13.refs_3_, ...), custom_call_target="tpu_custom_call" | custom-call | flops 3623878656 | bytes 18874368 | tf_op jit(solution)/shard_map/pallas_call | solution.py:357
  99.9 1.9 %collective-permute-done.22.refs_3_ = bf16[4,48,768]{2,1,0:T(8,128)(2,1)} collective-permute-done((bf16[4,48,768]{2,1,0:T(8,128)(2,1)}, bf16[4,48,768]{2,1,0:T(8,128)(2,1)}, u32[]{:S(2)}, u32[]{:S(2)}) %collective-permute-start.22) | collective-permute-done | bytes 294944 | tf_op jit(solution)/shard_map/ppermute | solution.py:49
  101.8 7.5 %shard_map.171 = (bf16[2,192,768]{2,1,0:T(8,128)(2,1)}, bf16[48,3072]{1,0:T(8,128)(2,1)}) custom-call(bf16[4,48,768]{2,1,0:T(8,128)(2,1)} %copy-done.22, bf16[4,48,768]{2,1,0:T(8,128)(2,1)} %copy-done.24, bf16[4,48,768]{2,1,0:T(8,128)(2,1)} %copy-done.25, bf16[4,48,768]{2,1,0:T(8,128)(2,1)} %collective-permute-done.22.refs_3_, f32[2,4,4,3072]{3,2,1,0:T(4,128)} %refs_4_.5, ...), custom_call_target="tpu_custom_call" | custom-call | flops 3623878656 | bytes 18874368 | tf_op jit(solution)/shard_map/pallas_call | solution.py:357
  110.1 4.2 %collective-permute-done.24.refs_1_.refs_3_ = bf16[2,192,768]{2,1,0:T(8,128)(2,1)S(1)} collective-permute-done((bf16[2,192,768]{2,1,0:T(8,128)(2,1)}, bf16[2,192,768]{2,1,0:T(8,128)(2,1)S(1)}, u32[]{:S(2)}, u32[]{:S(2)}) %collective-permute-start.24) | collective-permute-done | bytes 589856 | tf_op jit(solution)/shard_map/ppermute | solution.py:49
  115.1 5.3 %shard_map.172 = (bf16[1,48,768]{2,1,0:T(8,128)(2,1)}, bf16[1,48,768]{2,1,0:T(8,128)(2,1)}, bf16[1,48,768]{2,1,0:T(8,128)(2,1)}, bf16[1,48,768]{2,1,0:T(8,128)(2,1)}) custom-call(bf16[2,192,768]{2,1,0:T(8,128)(2,1)} %get-tuple-element.105.refs_0_.refs_2_, bf16[2,192,768]{2,1,0:T(8,128)(2,1)} %copy-done.1, bf16[3072,768]{1,0:T(8,128)(2,1)} %refs_2_.3), custom_call_target="tpu_custom_call" | custom-call | flops 905969664 | bytes 4718592 | tf_op jit(solution)/shard_map/pallas_call | solution.py:423
  120.4 6.5 %collective-permute-done.23.refs_1_ = bf16[2,192,768]{2,1,0:T(8,128)(2,1)S(1)} collective-permute-done((bf16[2,192,768]{2,1,0:T(8,128)(2,1)}, bf16[2,192,768]{2,1,0:T(8,128)(2,1)S(1)}, u32[]{:S(2)}, u32[]{:S(2)}) %collective-permute-start.23) | collective-permute-done | bytes 589856 | tf_op jit(solution)/shard_map/ppermute | solution.py:49
  127.7 5.5 %shard_map.173 = (bf16[2,48,768]{2,1,0:T(8,128)(2,1)}, bf16[2,48,768]{2,1,0:T(8,128)(2,1)}, bf16[2,48,768]{2,1,0:T(8,128)(2,1)}, bf16[2,48,768]{2,1,0:T(8,128)(2,1)}) custom-call(bf16[2,192,768]{2,1,0:T(8,128)(2,1)} %get-tuple-element.100.refs_0_, bf16[2,192,768]{2,1,0:T(8,128)(2,1)} %copy-done.2, bf16[3072,768]{1,0:T(8,128)(2,1)} %refs_2_.3, ...), custom_call_target="tpu_custom_call" | custom-call | flops 905969664 | bytes 4718592 | tf_op jit(solution)/shard_map/pallas_call | solution.py:423
  133.2 5.7 %collective-permute-done.28.refs_4_ = bf16[1536,768]{1,0:T(8,128)(2,1)} collective-permute-done((bf16[1536,768]{1,0:T(8,128)(2,1)}, bf16[1536,768]{1,0:T(8,128)(2,1)}, u32[]{:S(2)}, u32[]{:S(2)}) %collective-permute-start.28) | collective-permute-done | bytes 2359328 | tf_op jit(solution)/shard_map/ppermute | solution.py:57
  145.1 6.9 %shard_map.174 = (bf16[2,48,768]{2,1,0:T(8,128)(2,1)}, bf16[2,48,768]{2,1,0:T(8,128)(2,1)}, bf16[2,48,768]{2,1,0:T(8,128)(2,1)}, bf16[2,48,768]{2,1,0:T(8,128)(2,1)}) custom-call(bf16[2,192,768]{2,1,0:T(8,128)(2,1)} %get-tuple-element.100.refs_0_, bf16[2,192,768]{2,1,0:T(8,128)(2,1)} %copy-done.2, bf16[2,192,768]{2,1,0:T(8,128)(2,1)} %get-tuple-element.105.refs_0_.refs_2_, ...), custom_call_target="tpu_custom_call" | custom-call | flops 1811939328 | bytes 4718592 | tf_op jit(solution)/shard_map/pallas_call | solution.py:423
  153.7 2.9 %collective-permute-start.31 = (bf16[2,48,768]{2,1,0:T(8,128)(2,1)}, bf16[2,48,768]{2,1,0:T(8,128)(2,1)S(1)}, u32[]{:S(2)}, u32[]{:S(2)}) collective-permute-start(bf16[2,48,768]{2,1,0:T(8,128)(2,1)} %get-tuple-element.123), channel_id=1, source_target_pairs={{0,8},{4,12},{8,0},{12,4},{1,9},{5,13},{9,1},{13,5},{2,10},{6,14},... | collective-permute-start | bytes 442376 | tf_op jit(solution)/shard_map/ppermute | solution.py:76
  157.0 2.1 %collective-permute-done.30 = bf16[2,48,768]{2,1,0:T(8,128)(2,1)S(1)} collective-permute-done((bf16[2,48,768]{2,1,0:T(8,128)(2,1)}, bf16[2,48,768]{2,1,0:T(8,128)(2,1)S(1)}, u32[]{:S(2)}, u32[]{:S(2)}) %collective-permute-start.30) | collective-permute-done | bytes 147488 | tf_op jit(solution)/shard_map/ppermute | solution.py:76
  159.1 8.5 %collective-permute-done.31 = bf16[2,48,768]{2,1,0:T(8,128)(2,1)S(1)} collective-permute-done((bf16[2,48,768]{2,1,0:T(8,128)(2,1)}, bf16[2,48,768]{2,1,0:T(8,128)(2,1)S(1)}, u32[]{:S(2)}, u32[]{:S(2)}) %collective-permute-start.31) | collective-permute-done | bytes 147488 | tf_op jit(solution)/shard_map/ppermute | solution.py:76
  167.6 2.0 %collective-permute-done.32 = bf16[2,48,768]{2,1,0:T(8,128)(2,1)S(1)} collective-permute-done((bf16[2,48,768]{2,1,0:T(8,128)(2,1)}, bf16[2,48,768]{2,1,0:T(8,128)(2,1)S(1)}, u32[]{:S(2)}, u32[]{:S(2)}) %collective-permute-start.32) | collective-permute-done | bytes 147488 | tf_op jit(solution)/shard_map/ppermute | solution.py:76
  (120 shorter events, 45.8 us)
Async XLA Ops:
  5.4 14.4 %collective-permute-start = (bf16[384,384]{1,0:T(8,128)(2,1)}, bf16[384,384]{1,0:T(8,128)(2,1)S(1)}, u32[]{:S(2)}, u32[]{:S(2)}) collective-permute-start(bf16[384,384]{1,0:T(8,128)(2,1)} %constant_dynamic-slice_fusion.9), channel_id=1, source_target_pairs={{0,1},{1,0},{2,3},{3,2},{4,5},{5,4},{6,7},{7,6},{8,9},{9,8},{10,11... | collective-permute-start | bytes 884744 | tf_op jit(solution)/shard_map/ppermute | solution.py:49
  6.9 12.9 %collective-permute-start.1 = (bf16[384,384]{1,0:T(8,128)(2,1)}, bf16[384,384]{1,0:T(8,128)(2,1)S(1)}, u32[]{:S(2)}, u32[]{:S(2)}) collective-permute-start(bf16[384,384]{1,0:T(8,128)(2,1)} %constant_dynamic-slice_fusion.9), channel_id=1, source_target_pairs={{0,2},{1,3},{2,0},{3,1},{4,6},{5,7},{6,4},{7,5},{8,10},{9,11},{10,... | collective-permute-start | bytes 884744 | tf_op jit(solution)/shard_map/ppermute | solution.py:57
  8.4 9.1 %collective-permute-start.2 = (bf16[2,16,1536]{2,1,0:T(8,128)(2,1)}, bf16[2,16,1536]{2,1,0:T(8,128)(2,1)S(1)}, u32[]{:S(2)}, u32[]{:S(2)}) collective-permute-start(bf16[2,16,1536]{2,1,0:T(8,128)(2,1)} %shard_map.167.refs_0_), channel_id=1, source_target_pairs={{0,1},{1,0},{2,3},{3,2},{4,5},{5,4},{6,7},{7,6},{8,9},{9,8},{10,11... | collective-permute-start | bytes 294920 | tf_op jit(solution)/shard_map/ppermute | solution.py:69
  8.9 10.8 %collective-permute-start.3 = (bf16[2,16,1536]{2,1,0:T(8,128)(2,1)}, bf16[2,16,1536]{2,1,0:T(8,128)(2,1)S(1)}, u32[]{:S(2)}, u32[]{:S(2)}) collective-permute-start(bf16[2,16,1536]{2,1,0:T(8,128)(2,1)} %shard_map.167.refs_0_), channel_id=1, source_target_pairs={{0,2},{1,3},{2,0},{3,1},{4,6},{5,7},{6,4},{7,5},{8,10},{9,11},{10,... | collective-permute-start | bytes 294920 | tf_op jit(solution)/shard_map/ppermute | solution.py:69
  9.4 10.3 %collective-permute-start.4 = (bf16[2,16,1536]{2,1,0:T(8,128)(2,1)}, bf16[2,16,1536]{2,1,0:T(8,128)(2,1)}, u32[]{:S(2)}, u32[]{:S(2)}) collective-permute-start(bf16[2,16,1536]{2,1,0:T(8,128)(2,1)} %shard_map.167.refs_0_), channel_id=1, source_target_pairs={{0,3},{1,2},{2,1},{3,0},{4,7},{5,6},{6,5},{7,4},{8,11},{9,10},{10,... | collective-permute-start | bytes 294920 | tf_op jit(solution)/shard_map/ppermute | solution.py:69
  19.8 8.6 %collective-permute-start.8 = (bf16[384,384]{1,0:T(8,128)(2,1)S(1)}, bf16[384,384]{1,0:T(8,128)(2,1)S(1)}, u32[]{:S(2)}, u32[]{:S(2)}) collective-permute-start(bf16[384,384]{1,0:T(8,128)(2,1)S(1)} %collective-permute-done.refs_5_), channel_id=1, source_target_pairs={{0,2},{1,3},{2,0},{3,1},{4,6},{5,7},{6,4},{7,5},{8,10},{9,11},{10,... | collective-permute-start | bytes 884744 | tf_op jit(solution)/shard_map/ppermute | solution.py:57
  21.4 25.2 %collective-permute-start.10 = (bf16[768,768]{1,0:T(8,128)(2,1)S(1)}, bf16[768,768]{1,0:T(8,128)(2,1)}, u32[]{:S(2)}, u32[]{:S(2)}) collective-permute-start(bf16[768,768]{1,0:T(8,128)(2,1)S(1)} %get-tuple-element.78), channel_id=1, source_target_pairs={{0,1},{1,0},{2,3},{3,2},{4,5},{5,4},{6,7},{7,6},{8,9},{9,8},{10,11... | collective-permute-start | bytes 3538952 | tf_op jit(solution)/shard_map/ppermute | solution.py:49
  29.5 16.6 %collective-permute-start.9 = (bf16[1152,384]{1,0:T(8,128)(2,1)}, bf16[1152,384]{1,0:T(8,128)(2,1)}, u32[]{:S(2)}, u32[]{:S(2)}) collective-permute-start(bf16[1152,384]{1,0:T(8,128)(2,1)} %pad_maximum_fusion), channel_id=1, source_target_pairs={{0,16},{16,0},{1,17},{17,1},{2,18},{18,2},{3,19},{19,3},{4,20},{20... | collective-permute-start | bytes 2654216 | tf_op jit(solution)/shard_map/ppermute | solution.py:80
  29.5 6.3 %collective-permute-start.5 = (bf16[4,48,384]{2,1,0:T(8,128)(2,1)S(1)}, bf16[4,48,384]{2,1,0:T(8,128)(2,1)S(1)}, u32[]{:S(2)}, u32[]{:S(2)}) collective-permute-start(bf16[4,48,384]{2,1,0:T(8,128)(2,1)S(1)} %copy-done.8), channel_id=1, source_target_pairs={{0,4},{4,8},{8,12},{12,0},{1,5},{5,9},{9,13},{13,1},{2,6},{6,10},{... | collective-permute-start | bytes 442376 | tf_op jit(solution)/shard_map/ppermute | solution.py:76
  31.1 28.9 %collective-permute-start.16 = (bf16[768,768]{1,0:T(8,128)(2,1)S(1)}, bf16[768,768]{1,0:T(8,128)(2,1)}, u32[]{:S(2)}, u32[]{:S(2)}) collective-permute-start(bf16[768,768]{1,0:T(8,128)(2,1)S(1)} %get-tuple-element.77), channel_id=1, source_target_pairs={{0,2},{1,3},{2,0},{3,1},{4,6},{5,7},{6,4},{7,5},{8,10},{9,11},{10,... | collective-permute-start | bytes 3538952 | tf_op jit(solution)/shard_map/ppermute | solution.py:57
  32.4 11.9 %collective-permute-start.6 = (bf16[4,48,384]{2,1,0:T(8,128)(2,1)S(1)}, bf16[4,48,384]{2,1,0:T(8,128)(2,1)S(1)}, u32[]{:S(2)}, u32[]{:S(2)}) collective-permute-start(bf16[4,48,384]{2,1,0:T(8,128)(2,1)S(1)} %copy-done.8), channel_id=1, source_target_pairs={{0,8},{4,12},{8,0},{12,4},{1,9},{5,13},{9,1},{13,5},{2,10},{6,14},... | collective-permute-start | bytes 442376 | tf_op jit(solution)/shard_map/ppermute | solution.py:76
  35.7 10.4 %collective-permute-start.7 = (bf16[4,48,384]{2,1,0:T(8,128)(2,1)S(1)}, bf16[4,48,384]{2,1,0:T(8,128)(2,1)S(1)}, u32[]{:S(2)}, u32[]{:S(2)}) collective-permute-start(bf16[4,48,384]{2,1,0:T(8,128)(2,1)S(1)} %copy-done.8), channel_id=1, source_target_pairs={{0,12},{4,0},{8,4},{12,8},{1,13},{5,1},{9,5},{13,9},{2,14},{6,2},{... | collective-permute-start | bytes 442376 | tf_op jit(solution)/shard_map/ppermute | solution.py:76
  50.5 34.0 %collective-permute-start.17 = (bf16[768,768]{1,0:T(8,128)(2,1)}, bf16[768,768]{1,0:T(8,128)(2,1)S(1)}, u32[]{:S(2)}, u32[]{:S(2)}) collective-permute-start(bf16[768,768]{1,0:T(8,128)(2,1)} %collective-permute-done.10.refs_7_), channel_id=1, source_target_pairs={{0,2},{1,3},{2,0},{3,1},{4,6},{5,7},{6,4},{7,5},{8,10},{9,11},{10,... | collective-permute-start | bytes 3538952 | tf_op jit(solution)/shard_map/ppermute | solution.py:57
  51.8 22.0 %collective-permute-start.11 = (bf16[4,48,768]{2,1,0:T(8,128)(2,1)}, bf16[4,48,768]{2,1,0:T(8,128)(2,1)S(1)}, u32[]{:S(2)}, u32[]{:S(2)}) collective-permute-start(bf16[4,48,768]{2,1,0:T(8,128)(2,1)} %shard_map.169.refs_0_), channel_id=1, source_target_pairs={{0,4},{4,8},{8,12},{12,0},{1,5},{5,9},{9,13},{13,1},{2,6},{6,10},{... | collective-permute-start | bytes 884744 | tf_op jit(solution)/shard_map/ppermute | solution.py:76
  53.4 25.0 %collective-permute-start.12 = (bf16[4,48,768]{2,1,0:T(8,128)(2,1)}, bf16[4,48,768]{2,1,0:T(8,128)(2,1)S(1)}, u32[]{:S(2)}, u32[]{:S(2)}) collective-permute-start(bf16[4,48,768]{2,1,0:T(8,128)(2,1)} %shard_map.169.refs_0_), channel_id=1, source_target_pairs={{0,8},{4,12},{8,0},{12,4},{1,9},{5,13},{9,1},{13,5},{2,10},{6,14},... | collective-permute-start | bytes 884744 | tf_op jit(solution)/shard_map/ppermute | solution.py:76
  54.7 25.1 %collective-permute-start.13 = (bf16[4,48,768]{2,1,0:T(8,128)(2,1)}, bf16[4,48,768]{2,1,0:T(8,128)(2,1)}, u32[]{:S(2)}, u32[]{:S(2)}) collective-permute-start(bf16[4,48,768]{2,1,0:T(8,128)(2,1)} %shard_map.169.refs_0_), channel_id=1, source_target_pairs={{0,12},{4,0},{8,4},{12,8},{1,13},{5,1},{9,5},{13,9},{2,14},{6,2},{... | collective-permute-start | bytes 884744 | tf_op jit(solution)/shard_map/ppermute | solution.py:76
  60.0 19.7 %collective-permute-start.14 = (bf16[4,48,768]{2,1,0:T(8,128)(2,1)}, bf16[4,48,768]{2,1,0:T(8,128)(2,1)S(1)}, u32[]{:S(2)}, u32[]{:S(2)}) collective-permute-start(bf16[4,48,768]{2,1,0:T(8,128)(2,1)} %shard_map.169.refs_0_), channel_id=1, source_target_pairs={{0,1},{1,0},{2,3},{3,2},{4,5},{5,4},{6,7},{7,6},{8,9},{9,8},{10,11... | collective-permute-start | bytes 884744 | tf_op jit(solution)/shard_map/ppermute | solution.py:49
  73.8 6.7 %collective-permute-start.15 = (bf16[4,48,768]{2,1,0:T(8,128)(2,1)S(1)}, bf16[4,48,768]{2,1,0:T(8,128)(2,1)S(1)}, u32[]{:S(2)}, u32[]{:S(2)}) collective-permute-start(bf16[4,48,768]{2,1,0:T(8,128)(2,1)S(1)} %collective-permute-done.11.refs_1_), channel_id=1, source_target_pairs={{0,1},{1,0},{2,3},{3,2},{4,5},{5,4},{6,7},{7,6},{8,9},{9,8},{10,11... | collective-permute-start | bytes 884744 | tf_op jit(solution)/shard_map/ppermute | solution.py:49
  84.4 6.2 %collective-permute-start.19 = (bf16[768,768]{1,0:T(8,128)(2,1)}, bf16[768,768]{1,0:T(8,128)(2,1)}, u32[]{:S(2)}, u32[]{:S(2)}) collective-permute-start(bf16[768,768]{1,0:T(8,128)(2,1)} %collective-permute-done.16.refs_9_), channel_id=1, source_target_pairs={{0,16},{16,0},{1,17},{17,1},{2,18},{18,2},{3,19},{19,3},{4,20},{20... | collective-permute-start | bytes 3538952 | tf_op jit(solution)/shard_map/ppermute | solution.py:80
  84.9 5.8 %collective-permute-start.20 = (bf16[768,768]{1,0:T(8,128)(2,1)S(1)}, bf16[768,768]{1,0:T(8,128)(2,1)}, u32[]{:S(2)}, u32[]{:S(2)}) collective-permute-start(bf16[768,768]{1,0:T(8,128)(2,1)S(1)} %collective-permute-done.17.refs_11_), channel_id=1, source_target_pairs={{0,16},{16,0},{1,17},{17,1},{2,18},{18,2},{3,19},{19,3},{4,20},{20... | collective-permute-start | bytes 3538952 | tf_op jit(solution)/shard_map/ppermute | solution.py:80
  85.0 54.0 %collective-permute-start.28 = (bf16[1536,768]{1,0:T(8,128)(2,1)}, bf16[1536,768]{1,0:T(8,128)(2,1)}, u32[]{:S(2)}, u32[]{:S(2)}) collective-permute-start(bf16[1536,768]{1,0:T(8,128)(2,1)} %constant_dynamic-slice_fusion.6), channel_id=1, source_target_pairs={{0,2},{1,3},{2,0},{3,1},{4,6},{5,7},{6,4},{7,5},{8,10},{9,11},{10,... | collective-permute-start | bytes 7077896 | tf_op jit(solution)/shard_map/ppermute | solution.py:57
  86.2 13.7 %collective-permute-start.21 = (bf16[4,48,768]{2,1,0:T(8,128)(2,1)S(1)}, bf16[4,48,768]{2,1,0:T(8,128)(2,1)S(1)}, u32[]{:S(2)}, u32[]{:S(2)}) collective-permute-start(bf16[4,48,768]{2,1,0:T(8,128)(2,1)S(1)} %collective-permute-done.12.refs_2_), channel_id=1, source_target_pairs={{0,1},{1,0},{2,3},{3,2},{4,5},{5,4},{6,7},{7,6},{8,9},{9,8},{10,11... | collective-permute-start | bytes 884744 | tf_op jit(solution)/shard_map/ppermute | solution.py:49
  89.1 12.7 %collective-permute-start.22 = (bf16[4,48,768]{2,1,0:T(8,128)(2,1)}, bf16[4,48,768]{2,1,0:T(8,128)(2,1)}, u32[]{:S(2)}, u32[]{:S(2)}) collective-permute-start(bf16[4,48,768]{2,1,0:T(8,128)(2,1)} %collective-permute-done.13.refs_3_), channel_id=1, source_target_pairs={{0,1},{1,0},{2,3},{3,2},{4,5},{5,4},{6,7},{7,6},{8,9},{9,8},{10,11... | collective-permute-start | bytes 884744 | tf_op jit(solution)/shard_map/ppermute | solution.py:49
  98.3 15.9 %collective-permute-start.24 = (bf16[2,192,768]{2,1,0:T(8,128)(2,1)}, bf16[2,192,768]{2,1,0:T(8,128)(2,1)S(1)}, u32[]{:S(2)}, u32[]{:S(2)}) collective-permute-start(bf16[2,192,768]{2,1,0:T(8,128)(2,1)} %get-tuple-element.100.refs_0_), channel_id=1, source_target_pairs={{0,1},{1,0},{2,3},{3,2},{4,5},{5,4},{6,7},{7,6},{8,9},{9,8},{10,11... | collective-permute-start | bytes 1769480 | tf_op jit(solution)/shard_map/ppermute | solution.py:49
  109.3 17.6 %collective-permute-start.23 = (bf16[2,192,768]{2,1,0:T(8,128)(2,1)}, bf16[2,192,768]{2,1,0:T(8,128)(2,1)S(1)}, u32[]{:S(2)}, u32[]{:S(2)}) collective-permute-start(bf16[2,192,768]{2,1,0:T(8,128)(2,1)} %get-tuple-element.105.refs_0_.refs_2_), channel_id=1, source_target_pairs={{0,1},{1,0},{2,3},{3,2},{4,5},{5,4},{6,7},{7,6},{8,9},{9,8},{10,11... | collective-permute-start | bytes 1769480 | tf_op jit(solution)/shard_map/ppermute | solution.py:49
  138.9 4.7 %collective-permute-start.29 = (bf16[1536,768]{1,0:T(8,128)(2,1)}, bf16[1536,768]{1,0:T(8,128)(2,1)S(1)}, u32[]{:S(2)}, u32[]{:S(2)}) collective-permute-start(bf16[1536,768]{1,0:T(8,128)(2,1)} %collective-permute-done.28.refs_4_), channel_id=1, source_target_pairs={{0,16},{16,0},{1,17},{17,1},{2,18},{18,2},{3,19},{19,3},{4,20},{20... | collective-permute-start | bytes 7077896 | tf_op jit(solution)/shard_map/ppermute | solution.py:80
  139.7 16.8 %collective-permute-start.25 = (bf16[2,48,768]{2,1,0:T(8,128)(2,1)}, bf16[2,48,768]{2,1,0:T(8,128)(2,1)S(1)}, u32[]{:S(2)}, u32[]{:S(2)}) collective-permute-start(bf16[2,48,768]{2,1,0:T(8,128)(2,1)} %get-tuple-element.116), channel_id=1, source_target_pairs={{0,4},{4,8},{8,12},{12,0},{1,5},{5,9},{9,13},{13,1},{2,6},{6,10},{... | collective-permute-start | bytes 442376 | tf_op jit(solution)/shard_map/ppermute | solution.py:76
  141.4 15.2 %collective-permute-start.26 = (bf16[2,48,768]{2,1,0:T(8,128)(2,1)}, bf16[2,48,768]{2,1,0:T(8,128)(2,1)S(1)}, u32[]{:S(2)}, u32[]{:S(2)}) collective-permute-start(bf16[2,48,768]{2,1,0:T(8,128)(2,1)} %get-tuple-element.117), channel_id=1, source_target_pairs={{0,8},{4,12},{8,0},{12,4},{1,9},{5,13},{9,1},{13,5},{2,10},{6,14},... | collective-permute-start | bytes 442376 | tf_op jit(solution)/shard_map/ppermute | solution.py:76
  142.6 14.0 %collective-permute-start.27 = (bf16[2,48,768]{2,1,0:T(8,128)(2,1)}, bf16[2,48,768]{2,1,0:T(8,128)(2,1)S(1)}, u32[]{:S(2)}, u32[]{:S(2)}) collective-permute-start(bf16[2,48,768]{2,1,0:T(8,128)(2,1)} %get-tuple-element.118), channel_id=1, source_target_pairs={{0,12},{4,0},{8,4},{12,8},{1,13},{5,1},{9,5},{13,9},{2,14},{6,2},{... | collective-permute-start | bytes 442376 | tf_op jit(solution)/shard_map/ppermute | solution.py:76
  152.0 7.1 %collective-permute-start.30 = (bf16[2,48,768]{2,1,0:T(8,128)(2,1)}, bf16[2,48,768]{2,1,0:T(8,128)(2,1)S(1)}, u32[]{:S(2)}, u32[]{:S(2)}) collective-permute-start(bf16[2,48,768]{2,1,0:T(8,128)(2,1)} %get-tuple-element.122), channel_id=1, source_target_pairs={{0,4},{4,8},{8,12},{12,0},{1,5},{5,9},{9,13},{13,1},{2,6},{6,10},{... | collective-permute-start | bytes 442376 | tf_op jit(solution)/shard_map/ppermute | solution.py:76
  153.7 13.9 %collective-permute-start.31 = (bf16[2,48,768]{2,1,0:T(8,128)(2,1)}, bf16[2,48,768]{2,1,0:T(8,128)(2,1)S(1)}, u32[]{:S(2)}, u32[]{:S(2)}) collective-permute-start(bf16[2,48,768]{2,1,0:T(8,128)(2,1)} %get-tuple-element.123), channel_id=1, source_target_pairs={{0,8},{4,12},{8,0},{12,4},{1,9},{5,13},{9,1},{13,5},{2,10},{6,14},... | collective-permute-start | bytes 442376 | tf_op jit(solution)/shard_map/ppermute | solution.py:76
  156.6 13.1 %collective-permute-start.32 = (bf16[2,48,768]{2,1,0:T(8,128)(2,1)}, bf16[2,48,768]{2,1,0:T(8,128)(2,1)S(1)}, u32[]{:S(2)}, u32[]{:S(2)}) collective-permute-start(bf16[2,48,768]{2,1,0:T(8,128)(2,1)} %get-tuple-element.124), channel_id=1, source_target_pairs={{0,12},{4,0},{8,4},{12,8},{1,13},{5,1},{9,5},{13,9},{2,14},{6,2},{... | collective-permute-start | bytes 442376 | tf_op jit(solution)/shard_map/ppermute | solution.py:76
  (30 other events, 361.1 us)
